TPU v7x, 32 devices: a whole 2x2x4 slice. The times are simulated.
32 devices in a mesh: shots: 2 (over x), slab: 16 (over z, y, core).
Axes of the slice: x: 2, y: 2, z: 4, core: 2. Of those that a mesh axis runs over, the one named last changes fastest.
Arguments:
- fields: float32 [32, 2, 2, 128, 256], P(('shots', 'slab')), parts along dimension 0, may hold values from -6 to 6
- freq_index: int32 [32], P(('shots', 'slab')), parts along dimension 0, may hold values from 0 to 511
- slowness_index: int32 [16, 128, 256], P('slab'), may hold values from 0 to 255
- slowness_table: float32 [256], replicated, may hold values from 1.2 to 2.4
Outputs:
- image: float32 [32, 128, 256], P(('shots', 'slab')), parts along dimension 0
- fields_out: float32 [32, 2, 2, 128, 256], P(('shots', 'slab')), parts along dimension 0
There are 2 independent parts, one for each index of `shots`. A program takes and returns all parts, laid end to end along the dimension named above; an argument that names none is the same for every part. Nothing has to cross between parts.
All inputs are finite; a program needn't handle non-finite values.
Results may differ from a plain program's by a relative error of at most 0.0003.
Values sent between devices are 32-bit elements; how exact they have to be, the bound alone decides.
No kernel may reach another device: no remote copies, remote signals or barrier semaphores. Data moves between devices by JAX's collectives and lax.ppermute only.
A program may use at most 64 MiB of HBM per device.

v0:
```python
import functools
import math

import jax
import jax.numpy as jnp
import ml_dtypes
import numpy as np
from jax import lax
from jax.experimental import pallas as pl
from jax.experimental.pallas import tpu as pltpu
from jax.sharding import PartitionSpec as P

TICKS = 3
NFREQ = 512
EXTRA = 8
LANES = 128
TABLES = 5
TWO_PI = 2.0 * math.pi


def split_table(angle):
    parts = np.concatenate([np.cos(angle), np.sin(angle)], axis=0)
    high = parts.astype(np.float32).astype(ml_dtypes.bfloat16)
    low = (parts - high.astype(np.float64)).astype(np.float32).astype(ml_dtypes.bfloat16)
    return np.concatenate([high, low], axis=0)


def x_order(rows):
    front = np.arange(rows // 2)
    return np.concatenate([front, [rows // 2], rows - front[1:]])


def dft_tables(rows, cols):
    x_no, y_no = np.arange(rows), np.arange(cols // 2)
    to_x = np.outer(x_order(rows), x_no) % rows * (TWO_PI / rows)
    even = np.outer(y_no, 2 * y_no) % cols * (TWO_PI / cols)
    to_odd = np.outer(y_no, 2 * y_no + 1) % cols * (TWO_PI / cols)
    return [split_table(angle) for angle in (to_x, to_x.T, even, to_odd, to_odd.T)]


def passes(value, axis):
    high = value.astype(jnp.bfloat16)
    low = (value - high.astype(jnp.float32)).astype(jnp.bfloat16)
    return jnp.concatenate([high, low, high], axis=axis)


def table_parts(table_ref, turn):
    size = table_ref.shape[1]
    parts = []
    for start in (0, 2 * size):
        cos = table_ref[start : start + size]
        sin = table_ref[start + size : start + 2 * size]
        if turn:
            parts.append(stack(side(cos, sin), side(-sin, cos)))
        else:
            parts.append(stack(side(cos, -sin), side(sin, cos)))
    return parts


def dot_right(value, table_ref):
    high, low = table_parts(table_ref, False)
    return jnp.dot(
        passes(value, 1), stack(high, high, low), preferred_element_type=jnp.float32
    )


def dot_left(table_ref, value):
    high, low = table_parts(table_ref, True)
    return jnp.dot(side(high, high, low), passes(value, 0), preferred_element_type=jnp.float32)


def cos_sin(angle):
    turns = jnp.floor(angle * (1.0 / math.pi) + 0.5)
    pairs = turns * 0.5
    flip = 1.0 - 4.0 * (pairs - jnp.floor(pairs))
    rest = angle - turns * math.pi
    sq = rest * rest
    sin = -1.98089830e-4 + sq * 2.60501962e-6
    sin = 8.33304978e-3 + sq * sin
    sin = -1.66666579e-1 + sq * sin
    sin = 9.99999996e-1 + sq * sin
    cos = -1.38535979e-3 + sq * 2.31515763e-5
    cos = 4.16635698e-2 + sq * cos
    cos = -4.99999047e-1 + sq * cos
    cos = 9.99999953e-1 + sq * cos
    return cos * flip, sin * (rest * flip)


def wave_square(rows, cols):
    half = cols // 2
    shape = (rows // 2 + EXTRA, cols)
    row = lax.broadcasted_iota(jnp.int32, shape, 0)
    row = jnp.where(row > rows // 2, rows // 2 - row, row)
    col = lax.broadcasted_iota(jnp.int32, shape, 1)
    col = jnp.where(col < half, 2 * col, 2 * (col - half) + 1)
    col = jnp.where(col < half, col, col - cols)
    wave_x = row.astype(jnp.float32) * (TWO_PI / rows)
    wave_y = col.astype(jnp.float32) * (TWO_PI / cols)
    return wave_x * wave_x + wave_y * wave_y


def depth_factor(omega_mean, wave_sq, rows, cols):
    gap = omega_mean * omega_mean - wave_sq
    root = jnp.sqrt(jnp.abs(gap))
    cos, sin = cos_sin(root)
    scale = 1.0 / (rows * cols)
    wave = gap > 0.0
    cos = jnp.where(wave, cos, jnp.exp(-root)) * scale
    sin = jnp.where(wave, sin, 0.0) * scale
    return [stack(part, part[EXTRA : rows // 2]) for part in (cos, sin)]


def side(*parts):
    return jnp.concatenate(parts, axis=1)


def stack(*parts):
    return jnp.concatenate(parts, axis=0)


def depth_step(fields, factor, screen, tables):
    left, left_back, even, odd, odd_back = tables
    spectra = []
    for real, imag in fields:
        half = real.shape[1] // 2
        first = side(real[:, :half], imag[:, :half])
        second = side(real[:, half:], imag[:, half:])
        spectra.append((dot_right(first + second, even), dot_right(first - second, odd)))
    spectra = [
        stack(side(low[:, :half], high[:, :half]), side(low[:, half:], high[:, half:]))
        for low, high in spectra
    ]
    spectra = [dot_left(left, spectrum) for spectrum in spectra]
    cos, sin = factor()
    rows = cos.shape[0]
    moved = []
    for spectrum in spectra:
        real, imag = spectrum[:rows], spectrum[rows:]
        moved.append(stack(real * sin + imag * cos, real * cos - imag * sin))
    backs = [dot_left(left_back, spectrum) for spectrum in moved]
    parts = []
    for back in backs:
        sum_part = dot_right(side(back[:rows, :half], back[rows:, :half]), even)
        gap_part = dot_right(side(back[:rows, half:], back[rows:, half:]), odd_back)
        parts.append((sum_part, gap_part))
    cos, sin = screen()
    results = []
    for sum_part, gap_part in parts:
        first, second = sum_part + gap_part, sum_part - gap_part
        real = side(first[:, half:], second[:, half:])
        imag = side(first[:, :half], second[:, :half])
        results.append((real * cos - imag * sin, real * sin + imag * cos))
    return results


def both_fields(state_ref, rows, factor, screen, tables):
    def fields():
        if len(state_ref.shape) == 2:
            parts = [state_ref[i * rows : (i + 1) * rows] for i in range(4)]
        else:
            parts = [state_ref[0, i, j] for i in range(2) for j in range(2)]
        s_real, s_imag, r_real, r_imag = parts
        return (s_real, s_imag), (r_imag, r_real)

    (s_real, s_imag), (r_imag, r_real) = depth_step(fields(), factor, screen, tables)
    return (s_real, s_imag, r_real, r_imag), s_real * r_real + s_imag * r_imag


def look_up(index, *tables):
    found = []
    for table in tables:
        pieces = []
        for start in range(0, index.shape[1], LANES):
            piece = index[:, start : start + LANES]
            value = jnp.zeros(piece.shape, jnp.float32)
            for low in range(0, table.shape[1], LANES):
                entries = jnp.broadcast_to(table[:, low : low + LANES], piece.shape)
                inside = jnp.clip(piece - low, 0, LANES - 1)
                picked = jnp.take_along_axis(entries, inside, axis=1)
                value = jnp.where(piece >= low, picked, value)
            pieces.append(value)
        found.append(side(*pieces))
    return found


def screen_of(index, omega, entries, mean):
    return look_up(index, *cos_sin(omega * (entries - mean)))


def store_planes(ref, planes):
    rows = planes[0].shape[0]
    for i, plane in enumerate(planes):
        ref[i * rows : (i + 1) * rows] = plane


def is_odd():
    return lax.rem(lax.axis_index("slab"), 2) == 1


def is_even():
    return jnp.logical_not(is_odd())


def load_and_step(operands, outputs, scratch):
    freq_hbm, fields_hbm, index_hbm, entries_hbm, *tables_hbm = operands
    state_ref, plane_ref, image_ref, wave_ref, levels_ref, *tables = outputs
    freq_ref, own_ref, index_ref, entries_ref, sems = scratch
    rows, cols = image_ref.shape
    pairs = [(fields_hbm, own_ref), (index_hbm, index_ref), (entries_hbm, entries_ref)]
    pairs += [(freq_hbm, freq_ref), *zip(tables_hbm, tables)]
    copies = [pltpu.make_async_copy(*pair, sems.at[i]) for i, pair in enumerate(pairs)]
    for copy in copies:
        copy.start()
    wave_sq = wave_square(rows, cols)
    wave_ref[...] = wave_sq
    for copy in copies:
        copy.wait()
    index, entries = index_ref[0], entries_ref[...]
    omega = 1.0 + freq_ref[0].astype(jnp.float32) * (1.0 / NFREQ)
    means = []

    def factor():
        (slow,) = look_up(index, entries)
        means.append(jnp.sum(slow, axis=(0, 1), keepdims=True) * (1.0 / (rows * cols)))
        return depth_factor(omega * means[0], wave_sq, rows, cols)

    planes, image = both_fields(
        own_ref, rows, factor, lambda: screen_of(index, omega, entries, means[0]), tables
    )
    store_planes(state_ref, planes)
    state_ref[4 * rows :] = jnp.full((state_ref.shape[0] - 4 * rows, cols), omega, jnp.float32)
    image_ref[...] = image
    plane_ref[:rows] = index.astype(jnp.float32)
    plane_ref[rows:] = jnp.broadcast_to(means[0], (EXTRA, cols))
    levels_ref[...] = jnp.broadcast_to(entries, levels_ref.shape)


def odd_first_kernel(*refs):
    operands, refs = refs[: 4 + TABLES], refs[4 + TABLES :]
    outputs, scratch = refs[: 5 + TABLES], refs[5 + TABLES :]
    pl.when(is_odd())(functools.partial(load_and_step, operands, outputs, scratch))


def even_first_kernel(*refs):
    operands, refs = refs[: 4 + TABLES], refs[4 + TABLES :]
    kept, refs = refs[: 4 + TABLES], refs[4 + TABLES :]
    outputs, scratch = refs[: 5 + TABLES], refs[5 + TABLES :]
    pl.when(is_even())(functools.partial(load_and_step, operands, outputs, scratch))

    @pl.when(is_odd())
    def _():
        for kept_ref, out_ref in zip(kept, outputs[1:]):
            out_ref[...] = kept_ref[...]


def step_from(state_ref, plane_ref, constants):
    wave_ref, levels_ref, *tables = constants
    rows = plane_ref.shape[0] - EXTRA
    omega = state_ref[4 * rows : 4 * rows + 1, :1]
    mean = plane_ref[rows : rows + 1, :1]
    index = plane_ref[:rows].astype(jnp.int32)
    return both_fields(
        state_ref,
        rows,
        lambda: depth_factor(omega * mean, wave_ref[...], rows, index.shape[1]),
        lambda: screen_of(index, omega, levels_ref[:1], mean),
        tables,
    )


def odd_second_kernel(state_in_ref, plane_ref, image_in_ref, *refs):
    constants, (state_ref, image_ref) = refs[: 2 + TABLES], refs[2 + TABLES :]
    rows = image_ref.shape[0]

    @pl.when(is_odd())
    def _():
        planes, image = step_from(state_in_ref, plane_ref, constants)
        store_planes(state_ref, planes)
        for start in range(4 * rows, state_ref.shape[0], EXTRA):
            state_ref[start : start + EXTRA] = state_in_ref[4 * rows :]
        image_ref[...] = image_in_ref[...] + image

    @pl.when(is_even())
    def _():
        image_ref[...] = image_in_ref[...]


def odd_ahead_kernel(state_in_ref, plane_ref, *refs):
    constants, (image_ref,) = refs[: 2 + TABLES], refs[2 + TABLES :]
    has_next = is_odd() & (lax.axis_index("slab") < lax.axis_size("slab") - 1)

    @pl.when(has_next)
    def _():
        _, image = step_from(state_in_ref, plane_ref, constants)
        image_ref[...] = image

    @pl.when(jnp.logical_not(has_next))
    def _():
        image_ref[...] = jnp.zeros_like(image_ref)


def fill_wide(ref, raw):
    rows = raw.shape[0]
    ref[:rows] = raw
    ref[rows:] = jnp.zeros((ref.shape[0] - rows, ref.shape[1]), jnp.float32)


def even_arrival_kernel(state_in_ref, plane_ref, image_in_ref, *refs):
    constants, (state_ref, image_ref, up_ref) = refs[: 2 + TABLES], refs[2 + TABLES :]
    rows = image_ref.shape[0]

    @pl.when(is_even())
    def _():
        planes, image = step_from(state_in_ref, plane_ref, constants)
        store_planes(state_ref, planes)
        state_ref[4 * rows :] = state_in_ref[4 * rows : 4 * rows + EXTRA]
        image = image_in_ref[...] + image
        image_ref[...] = image
        fill_wide(up_ref, image)

    @pl.when(is_odd())
    def _():
        image_ref[...] = image_in_ref[...]


def odd_last_kernel(state_in_ref, plane_ref, image_in_ref, ahead_ref, *refs):
    constants, (state_ref, raw_ref, base_ref) = refs[: 2 + TABLES], refs[2 + TABLES :]

    @pl.when(is_odd())
    def _():
        planes, image = step_from(state_in_ref, plane_ref, constants)
        store_planes(state_ref, planes)
        raw = image_in_ref[...] + image
        fill_wide(raw_ref, raw)
        base_ref[...] = raw - 0.25 * ahead_ref[...]


def even_last_kernel(
    state_in_ref, plane_ref, image_in_ref, odd_raw_ref, odd_base_ref, *refs
):
    constants, (state_ref, raw_ref, base_ref) = refs[: 2 + TABLES], refs[2 + TABLES :]

    @pl.when(is_even())
    def _():
        planes, image = step_from(state_in_ref, plane_ref, constants)
        store_planes(state_ref, planes)
        raw = image_in_ref[...] + image
        raw_ref[...] = raw
        base_ref[...] = raw

    @pl.when(is_odd())
    def _():
        raw_ref[...] = odd_raw_ref[: raw_ref.shape[0]]
        base_ref[...] = odd_base_ref[...]


def write_kernel(odd_ref, even_ref, fields_hbm, done_ref, sems):
    rows = even_ref.shape[0] // 4

    def write(ref):
        copies = [
            pltpu.make_async_copy(
                ref.at[pl.ds(i * rows, rows)], fields_hbm.at[0, i // 2, i % 2], sems.at[i]
            )
            for i in range(4)
        ]
        for copy in copies:
            copy.start()
        for copy in copies:
            copy.wait()

    pl.when(is_odd())(functools.partial(write, odd_ref))
    pl.when(is_even())(functools.partial(write, even_ref))
    done_ref[...] = jnp.zeros_like(done_ref)


def stencil_kernel(base_ref, below_ref, above_ref, swap_ref, done_ref, image_ref):
    del done_ref
    rows = base_ref.shape[0]
    off = below_ref[:rows] + above_ref[:rows]
    image_ref[0] = base_ref[...] - 0.25 * (swap_ref[...] + off)


def body(fields, freq_index, slowness_index, slowness_table):
    rows, cols = slowness_index.shape[1:]
    slabs = lax.axis_size("slab")
    on_pairs = [(i, i + 1) for i in range(0, slabs - 1, 2)]
    off_pairs = [(i, i + 1) for i in range(1, slabs - 1, 2)]
    on_back = [(j, i) for i, j in on_pairs]
    off_back = [(j, i) for i, j in off_pairs]

    f32 = jnp.float32
    vmem = pl.BlockSpec(memory_space=pltpu.VMEM)
    hbm = pl.BlockSpec(memory_space=pltpu.HBM)
    products = 24 * (2 * rows) * cols * cols
    cost = pl.CostEstimate(flops=2 * products, bytes_accessed=16 * rows * cols * 4, transcendentals=0)

    long = pl.CostEstimate(
        flops=10 * 2 * products, bytes_accessed=10 * 16 * rows * cols * 4, transcendentals=0
    )

    def shape_of(height):
        return jax.ShapeDtypeStruct((height, cols), f32)

    def call(kernel, name, operands, out_shapes, cost=cost, **rest):
        rest.setdefault("in_specs", [vmem] * len(operands))
        rest.setdefault("out_specs", (vmem,) * len(out_shapes))
        return pl.pallas_call(
            kernel,
            out_shape=tuple(out_shapes),
            compiler_params=pltpu.CompilerParams(vmem_limit_bytes=32 * 1024 * 1024),
            cost_estimate=cost,
            name=name,
            **rest,
        )(*operands)

    long_state_shape = shape_of(4 * rows + 2 * EXTRA)
    state_shape, plane_shape, image_shape = shape_of(4 * rows + EXTRA), shape_of(rows + EXTRA), shape_of(rows)
    tables = [jnp.asarray(table) for table in dft_tables(rows, cols)]
    table_shapes = [jax.ShapeDtypeStruct(t.shape, t.dtype) for t in tables]
    levels_shape = jax.ShapeDtypeStruct((EXTRA,) + slowness_table.shape, f32)
    kept_shapes = [plane_shape, image_shape, shape_of(rows // 2 + EXTRA), levels_shape] + table_shapes
    loaded = (fields, slowness_index, slowness_table[None], *tables)
    operands = (freq_index,) + tuple(
        pltpu.with_memory_space_constraint(x, pltpu.HBM) for x in loaded
    )
    scratch = [
        pltpu.SMEM(freq_index.shape, freq_index.dtype),
        pltpu.VMEM(fields.shape, f32),
        pltpu.VMEM(slowness_index.shape, slowness_index.dtype),
        pltpu.VMEM((1,) + slowness_table.shape, f32),
        pltpu.SemaphoreType.DMA((4 + TABLES,)),
    ]
    odd_state, *kept = call(
        odd_first_kernel, "odd_first_step", operands, [long_state_shape] + kept_shapes,
        in_specs=[hbm] * len(operands), scratch_shapes=scratch,
    )
    from_off = lax.ppermute(odd_state, "slab", off_pairs)
    even_state, plane, image, *constants = call(
        even_first_kernel, "even_first_step", (*operands, *kept), [state_shape] + kept_shapes,
        in_specs=[hbm] * len(operands) + [vmem] * len(kept), scratch_shapes=scratch,
    )
    from_on = lax.ppermute(even_state, "slab", on_pairs)
    next_plane = lax.ppermute(plane, "slab", off_back)
    odd_state, image = call(
        odd_second_kernel, "odd_second_step", (from_on, plane, image, *constants),
        [shape_of(4 * rows + 3 * EXTRA), image_shape], cost=None,
    )
    last_off = lax.ppermute(odd_state, "slab", off_pairs)
    even_state, image, up_image = call(
        even_arrival_kernel, "even_arrival_step", (from_off, plane, image, *constants),
        [state_shape, image_shape, shape_of(rows + 2 * EXTRA)],
    )
    last_on = lax.ppermute(even_state, "slab", on_pairs)
    below = lax.ppermute(up_image, "slab", off_back)
    (ahead,) = call(
        odd_ahead_kernel, "odd_step_ahead", (odd_state, next_plane, *constants), [image_shape],
        cost=long,
    )
    odd_fields, odd_raw, odd_base = call(
        odd_last_kernel, "odd_last_step", (last_on, plane, image, ahead, *constants),
        [shape_of(4 * rows), shape_of(rows + EXTRA), image_shape], cost=None,
    )
    above = lax.ppermute(odd_raw, "slab", off_pairs)
    even_fields, raw, base = call(
        even_last_kernel, "even_last_step",
        (last_off, plane, image, odd_raw, odd_base, *constants),
        [shape_of(4 * rows), image_shape, image_shape], cost=None,
    )
    swapped = lax.ppermute(raw, "slab", on_pairs + on_back)
    fields_out, done = call(
        write_kernel, "write_fields", (odd_fields, even_fields),
        [jax.ShapeDtypeStruct(fields.shape, f32), jax.ShapeDtypeStruct((EXTRA, LANES), f32)],
        out_specs=(hbm, vmem), scratch_shapes=[pltpu.SemaphoreType.DMA((4,))], cost=None,
    )
    (image,) = call(
        stencil_kernel, "image_stencil", (base, below, above, swapped, done),
        [jax.ShapeDtypeStruct((1, rows, cols), f32)], cost=None,
    )
    return image, fields_out


def solution(mesh):
    return jax.shard_map(
        body,
        mesh=mesh,
        in_specs=(
            P(("shots", "slab"), None, None, None, None),
            P(("shots", "slab")),
            P("slab", None, None),
            P(),
        ),
        out_specs=(P(("shots", "slab"), None, None), P(("shots", "slab"), None, None, None, None)),
        check_vma=False,
    )
```

profile of v0, /device:TPU:10, one launch (start us, length us, event | category | flops | bytes accessed | tf_op | source)
XLA Modules:
  0.0 25.6 jit_solution(17791093932327012301)
XLA Ops:
  1.3 0.1 odd_first_step.1
  1.4 1.3 %collective-permute-start.2 = (f32[528,256]{1,0:T(8,128)S(1)}, f32[528,256]{1,0:T(8,128)S(1)}, u32[]{:S(2)}, u32[]{:S(2)}) collective-permute-start(f32[528,256]{1,0:T(8,128)S(1)} %get-tuple-element.55), channel_id=1, source_target_pairs={{1,2},{3,4},{5,6},{7,8},{9,10},{11,12},{13,14},{17,18},{19,20},{21... | collective-permute-start | bytes 1622024 | tf_op jit(solution)/shard_map/ppermute | solution.py:438
  2.7 2.8 %even_first_step.1 = (f32[520,256]{1,0:T(8,128)S(1)}, f32[136,256]{1,0:T(8,128)S(1)}, f32[128,256]{1,0:T(8,128)S(1)}, f32[72,256]{1,0:T(8,128)S(1)}, f32[8,256]{...) custom-call(s32[1]{0:T(128)S(6)} %copy.11.refs_0_, ...), custom_call_target="tpu_custom_call" | custom-call | flops 805306368 | bytes 2097152 | tf_op jit(solution)/shard_map/even_first_step/pallas_call | solution.py:408
  5.4 1.9 %collective-permute-start = (f32[520,256]{1,0:T(8,128)S(1)}, f32[520,256]{1,0:T(8,128)S(1)}, u32[]{:S(2)}, u32[]{:S(2)}) collective-permute-start(f32[520,256]{1,0:T(8,128)S(1)} %get-tuple-element.44), channel_id=1, source_target_pairs={{0,1},{2,3},{4,5},{6,7},{8,9},{10,11},{12,13},{14,15},{16,17},{18,... | collective-permute-start | bytes 1597448 | tf_op jit(solution)/shard_map/ppermute | solution.py:443
  7.4 2.3 %collective-permute-start.4 = (f32[136,256]{1,0:T(8,128)S(1)}, f32[136,256]{1,0:T(8,128)S(1)}, u32[]{:S(2)}, u32[]{:S(2)}) collective-permute-start(f32[136,256]{1,0:T(8,128)S(1)} %get-tuple-element.45.plane_ref), channel_id=1, source_target_pairs={{2,1},{4,3},{6,5},{8,7},{10,9},{12,11},{14,13},{18,17},{20,19},{22... | collective-permute-start | bytes 417800 | tf_op jit(solution)/shard_map/ppermute | solution.py:444
  9.7 0.0 collective-permute-done.state_in_ref
  9.7 1.3 %collective-permute-start.1 = (f32[536,256]{1,0:T(8,128)S(1)}, f32[536,256]{1,0:T(8,128)S(1)}, u32[]{:S(2)}, u32[]{:S(2)}) collective-permute-start(f32[536,256]{1,0:T(8,128)S(1)} %get-tuple-element.54.state_in_ref), channel_id=1, source_target_pairs={{1,2},{3,4},{5,6},{7,8},{9,10},{11,12},{13,14},{17,18},{19,20},{21... | collective-permute-start | bytes 1646600 | tf_op jit(solution)/shard_map/ppermute | solution.py:449
  11.0 2.3 %collective-permute-done.2.state_in_ref = f32[528,256]{1,0:T(8,128)S(1)} collective-permute-done((f32[528,256]{1,0:T(8,128)S(1)}, f32[528,256]{1,0:T(8,128)S(1)}, u32[]{:S(2)}, u32[]{:S(2)}) %collective-permute-start.2) | collective-permute-done | bytes 540704 | tf_op jit(solution)/shard_map/ppermute | solution.py:438
  13.4 1.3 %even_arrival_step.1 = (f32[520,256]{1,0:T(8,128)S(1)}, f32[128,256]{1,0:T(8,128)S(1)}, f32[144,256]{1,0:T(8,128)S(1)}) custom-call(f32[528,256]{1,0:T(8,128)S(1)} %collective-permute-done.2.state_in_ref, f32[136,256]{1,0:T(8,128)S(1)} %get-tuple-element.45.plane_ref, f32[128,256]{1,0:T(8,128)S(1)} %get-tuple-element.56.image_in_ref, ...), custom_call_target="tpu_custom_call" | custom-call | flops 805306368 | bytes 2097152 | tf_op jit(solution)/shard_map/even_arrival_step/pallas_call | solution.py:408
  14.7 1.3 %collective-permute-start.3 = (f32[520,256]{1,0:T(8,128)S(1)}, f32[520,256]{1,0:T(8,128)S(1)}, u32[]{:S(2)}, u32[]{:S(2)}) collective-permute-start(f32[520,256]{1,0:T(8,128)S(1)} %get-tuple-element.58), channel_id=1, source_target_pairs={{0,1},{2,3},{4,5},{6,7},{8,9},{10,11},{12,13},{14,15},{16,17},{18,... | collective-permute-start | bytes 1597448 | tf_op jit(solution)/shard_map/ppermute | solution.py:454
  16.0 1.5 %collective-permute-start.5 = (f32[144,256]{1,0:T(8,128)S(1)}, f32[144,256]{1,0:T(8,128)S(1)}, u32[]{:S(2)}, u32[]{:S(2)}) collective-permute-start(f32[144,256]{1,0:T(8,128)S(1)} %get-tuple-element.62), channel_id=1, source_target_pairs={{2,1},{4,3},{6,5},{8,7},{10,9},{12,11},{14,13},{18,17},{20,19},{22... | collective-permute-start | bytes 442376 | tf_op jit(solution)/shard_map/ppermute | solution.py:455
  17.6 0.0 collective-permute-done.4.plane_ref
  17.6 0.0 collective-permute-done.3.state_in_ref
  17.7 1.3 %collective-permute-start.6 = (f32[136,256]{1,0:T(8,128)S(1)}, f32[136,256]{1,0:T(8,128)S(1)}, u32[]{:S(2)}, u32[]{:S(2)}) collective-permute-start(f32[136,256]{1,0:T(8,128)S(1)} %get-tuple-element.59.odd_raw_ref), channel_id=1, source_target_pairs={{1,2},{3,4},{5,6},{7,8},{9,10},{11,12},{13,14},{17,18},{19,20},{21... | collective-permute-start | bytes 417800 | tf_op jit(solution)/shard_map/ppermute | solution.py:464
  19.0 2.5 %collective-permute-done.1.state_in_ref = f32[536,256]{1,0:T(8,128)S(1)} collective-permute-done((f32[536,256]{1,0:T(8,128)S(1)}, f32[536,256]{1,0:T(8,128)S(1)}, u32[]{:S(2)}, u32[]{:S(2)}) %collective-permute-start.1) | collective-permute-done | bytes 548896 | tf_op jit(solution)/shard_map/ppermute | solution.py:449
  21.5 1.3 %even_last_step.1 = (f32[512,256]{1,0:T(8,128)S(1)}, f32[128,256]{1,0:T(8,128)S(1)}, f32[128,256]{1,0:T(8,128)S(1)}) custom-call(f32[536,256]{1,0:T(8,128)S(1)} %collective-permute-done.1.state_in_ref, f32[136,256]{1,0:T(8,128)S(1)} %get-tuple-element.45.plane_ref, f32[128,256]{1,0:T(8,128)S(1)} %get-tuple-element.57.image_in_ref, ...), custom_call_target="tpu_custom_call" | custom-call | tf_op jit(solution)/shard_map/even_last_step/pallas_call | solution.py:408
  22.8 0.1 collective-permute-start.7
  22.9 0.8 %write_fields.1 = (f32[1,2,2,128,256]{4,3,2,1,0:T(8,128)}, f32[8,128]{1,0:T(8,128)S(1)}) custom-call(f32[512,256]{1,0:T(8,128)S(1)} %get-tuple-element.64.odd_ref, f32[512,256]{1,0:T(8,128)S(1)} %get-tuple-element.65.even_ref), custom_call_target="tpu_custom_call" | custom-call | tf_op jit(solution)/shard_map/write_fields/pallas_call | solution.py:408
  23.8 0.0 collective-permute-done.5.below_ref
  23.8 0.5 %collective-permute-done.7.swap_ref = f32[128,256]{1,0:T(8,128)S(1)} collective-permute-done((f32[128,256]{1,0:T(8,128)S(1)}, f32[128,256]{1,0:T(8,128)S(1)}, u32[]{:S(2)}, u32[]{:S(2)}) %collective-permute-start.7) | collective-permute-done | bytes 131104 | tf_op jit(solution)/shard_map/ppermute | solution.py:470
  24.2 0.7 %collective-permute-done.6.above_ref = f32[136,256]{1,0:T(8,128)S(1)} collective-permute-done((f32[136,256]{1,0:T(8,128)S(1)}, f32[136,256]{1,0:T(8,128)S(1)}, u32[]{:S(2)}, u32[]{:S(2)}) %collective-permute-start.6) | collective-permute-done | bytes 139296 | tf_op jit(solution)/shard_map/ppermute | solution.py:464
  24.9 0.7 %image_stencil.1 = f32[1,128,256]{2,1,0:T(8,128)} custom-call(f32[128,256]{1,0:T(8,128)S(1)} %get-tuple-element.61.base_ref, f32[144,256]{1,0:T(8,128)S(1)} %collective-permute-done.5.below_ref, f32[136,256]{1,0:T(8,128)S(1)} %collective-permute-done.6.above_ref, f32[128,256]{1,0:T(8,128)S(1)} %collective-permute-done.7.swap_ref, ...), custom_call_target="tpu_custom_call" | custom-call | tf_op jit(solution)/shard_map/image_stencil/pallas_call | solution.py:408
  (3 shorter events, 0.1 us)
Async XLA Ops:
  1.4 12.0 %collective-permute-start.2 = (f32[528,256]{1,0:T(8,128)S(1)}, f32[528,256]{1,0:T(8,128)S(1)}, u32[]{:S(2)}, u32[]{:S(2)}) collective-permute-start(f32[528,256]{1,0:T(8,128)S(1)} %get-tuple-element.55), channel_id=1, source_target_pairs={{1,2},{3,4},{5,6},{7,8},{9,10},{11,12},{13,14},{17,18},{19,20},{21... | collective-permute-start | bytes 1622024 | tf_op jit(solution)/shard_map/ppermute | solution.py:438
  5.4 4.2 %collective-permute-start = (f32[520,256]{1,0:T(8,128)S(1)}, f32[520,256]{1,0:T(8,128)S(1)}, u32[]{:S(2)}, u32[]{:S(2)}) collective-permute-start(f32[520,256]{1,0:T(8,128)S(1)} %get-tuple-element.44), channel_id=1, source_target_pairs={{0,1},{2,3},{4,5},{6,7},{8,9},{10,11},{12,13},{14,15},{16,17},{18,... | collective-permute-start | bytes 1597448 | tf_op jit(solution)/shard_map/ppermute | solution.py:443
  7.4 10.2 %collective-permute-start.4 = (f32[136,256]{1,0:T(8,128)S(1)}, f32[136,256]{1,0:T(8,128)S(1)}, u32[]{:S(2)}, u32[]{:S(2)}) collective-permute-start(f32[136,256]{1,0:T(8,128)S(1)} %get-tuple-element.45.plane_ref), channel_id=1, source_target_pairs={{2,1},{4,3},{6,5},{8,7},{10,9},{12,11},{14,13},{18,17},{20,19},{22... | collective-permute-start | bytes 417800 | tf_op jit(solution)/shard_map/ppermute | solution.py:444
  9.7 11.8 %collective-permute-start.1 = (f32[536,256]{1,0:T(8,128)S(1)}, f32[536,256]{1,0:T(8,128)S(1)}, u32[]{:S(2)}, u32[]{:S(2)}) collective-permute-start(f32[536,256]{1,0:T(8,128)S(1)} %get-tuple-element.54.state_in_ref), channel_id=1, source_target_pairs={{1,2},{3,4},{5,6},{7,8},{9,10},{11,12},{13,14},{17,18},{19,20},{21... | collective-permute-start | bytes 1646600 | tf_op jit(solution)/shard_map/ppermute | solution.py:449
  14.7 2.9 %collective-permute-start.3 = (f32[520,256]{1,0:T(8,128)S(1)}, f32[520,256]{1,0:T(8,128)S(1)}, u32[]{:S(2)}, u32[]{:S(2)}) collective-permute-start(f32[520,256]{1,0:T(8,128)S(1)} %get-tuple-element.58), channel_id=1, source_target_pairs={{0,1},{2,3},{4,5},{6,7},{8,9},{10,11},{12,13},{14,15},{16,17},{18,... | collective-permute-start | bytes 1597448 | tf_op jit(solution)/shard_map/ppermute | solution.py:454
  16.0 7.7 %collective-permute-start.5 = (f32[144,256]{1,0:T(8,128)S(1)}, f32[144,256]{1,0:T(8,128)S(1)}, u32[]{:S(2)}, u32[]{:S(2)}) collective-permute-start(f32[144,256]{1,0:T(8,128)S(1)} %get-tuple-element.62), channel_id=1, source_target_pairs={{2,1},{4,3},{6,5},{8,7},{10,9},{12,11},{14,13},{18,17},{20,19},{22... | collective-permute-start | bytes 442376 | tf_op jit(solution)/shard_map/ppermute | solution.py:455
  17.7 7.3 %collective-permute-start.6 = (f32[136,256]{1,0:T(8,128)S(1)}, f32[136,256]{1,0:T(8,128)S(1)}, u32[]{:S(2)}, u32[]{:S(2)}) collective-permute-start(f32[136,256]{1,0:T(8,128)S(1)} %get-tuple-element.59.odd_raw_ref), channel_id=1, source_target_pairs={{1,2},{3,4},{5,6},{7,8},{9,10},{11,12},{13,14},{17,18},{19,20},{21... | collective-permute-start | bytes 417800 | tf_op jit(solution)/shard_map/ppermute | solution.py:464
  22.8 1.4 %collective-permute-start.7 = (f32[128,256]{1,0:T(8,128)S(1)}, f32[128,256]{1,0:T(8,128)S(1)}, u32[]{:S(2)}, u32[]{:S(2)}) collective-permute-start(f32[128,256]{1,0:T(8,128)S(1)} %get-tuple-element.63), channel_id=1, source_target_pairs={{0,1},{2,3},{4,5},{6,7},{8,9},{10,11},{12,13},{14,15},{1,0},{3,2},... | collective-permute-start | bytes 393224 | tf_op jit(solution)/shard_map/ppermute | solution.py:470
where the time goes:
time: 25.9 us; the launch traced here: 25.6 us
  starting transfers between devices  11 us (42%)
  Pallas kernels  7.14 us (28%)
  waiting for transfers between devices  6.04 us (23%)
  between operations  1.44 us (6%)
    pallas_call x9, Pallas kernels, call(): pl.pallas_call(kernel, out_shape=tuple(out_shapes), compiler_params=pltpu...  7.14 us
    ppermute x1, waiting for transfers between devices, body(): last_off = lax.ppermute(odd_state, 'slab', off_pairs)  2.52 us
    ppermute x1, waiting for transfers between devices, body(): from_off = lax.ppermute(odd_state, 'slab', off_pairs)  2.34 us
    ppermute x1, starting transfers between devices, body(): next_plane = lax.ppermute(plane, 'slab', off_back)  2.3 us
    ppermute x1, starting transfers between devices, body(): from_on = lax.ppermute(even_state, 'slab', on_pairs)  1.91 us
    ppermute x1, starting transfers between devices, body(): below = lax.ppermute(up_image, 'slab', off_back)  1.53 us
    ppermute x1, starting transfers between devices, body(): last_on = lax.ppermute(even_state, 'slab', on_pairs)  1.32 us
    ppermute x1, starting transfers between devices, body(): from_off = lax.ppermute(odd_state, 'slab', off_pairs)  1.29 us
  transfers between devices with their start and end apart: 8, of which 4 were waited for; matrix products, arithmetic and copies ran while one was open for 0% of the time, Pallas kernels for 25%

commit v1 on v0

--- a/solution.py
+++ b/solution.py
@@ -14,7 +14,7 @@
 NFREQ = 512
 EXTRA = 8
 LANES = 128
-TABLES = 5
+TABLES = 2
 TWO_PI = 2.0 * math.pi
 
 
@@ -35,7 +35,16 @@
     to_x = np.outer(x_order(rows), x_no) % rows * (TWO_PI / rows)
     even = np.outer(y_no, 2 * y_no) % cols * (TWO_PI / cols)
     to_odd = np.outer(y_no, 2 * y_no + 1) % cols * (TWO_PI / cols)
-    return [split_table(angle) for angle in (to_x, to_x.T, even, to_odd, to_odd.T)]
+    groups = ((to_x, to_x.T), (even, to_odd, to_odd.T))
+    return [np.concatenate([split_table(angle) for angle in group]) for group in groups]
+
+
+def table_views(x_ref, y_ref):
+    views = []
+    for ref, count in ((x_ref, 2), (y_ref, 3)):
+        size = 4 * ref.shape[1]
+        views += [ref.at[pl.ds(i * size, size)] for i in range(count)]
+    return views
 
 
 def passes(value, axis):
@@ -119,7 +128,7 @@
 
 
 def depth_step(fields, factor, screen, tables):
-    left, left_back, even, odd, odd_back = tables
+    left, left_back, even, odd, odd_back = table_views(*tables)
     spectra = []
     for real, imag in fields:
         half = real.shape[1] // 2

time: 25.9 us -> 25.8 us (level)
  no operation moved by 1% of the time
where the time goes in v1:
time: 25.8 us; the launch traced here: 25.5 us
  starting transfers between devices  10.9 us (42%)
  Pallas kernels  7.18 us (28%)
  waiting for transfers between devices  6.05 us (23%)
  between operations  1.44 us (6%)
    pallas_call x9, Pallas kernels, call(): pl.pallas_call(kernel, out_shape=tuple(out_shapes), compiler_params=pltpu...  7.18 us
    ppermute x1, waiting for transfers between devices, body(): last_off = lax.ppermute(odd_state, 'slab', off_pairs)  2.53 us
    ppermute x1, waiting for transfers between devices, body(): from_off = lax.ppermute(odd_state, 'slab', off_pairs)  2.37 us
    ppermute x1, starting transfers between devices, body(): next_plane = lax.ppermute(plane, 'slab', off_back)  2.28 us
    ppermute x1, starting transfers between devices, body(): from_on = lax.ppermute(even_state, 'slab', on_pairs)  1.86 us
    ppermute x1, starting transfers between devices, body(): below = lax.ppermute(up_image, 'slab', off_back)  1.47 us
    ppermute x1, starting transfers between devices, body(): last_on = lax.ppermute(even_state, 'slab', on_pairs)  1.32 us
    ppermute x1, starting transfers between devices, body(): above = lax.ppermute(odd_raw, 'slab', off_pairs)  1.29 us
  transfers between devices with their start and end apart: 8, of which 4 were waited for; matrix products, arithmetic and copies ran while one was open for 0% of the time, Pallas kernels for 25%

profile of v1, /device:TPU:10, one launch (start us, length us, event | category | flops | bytes accessed | tf_op | source)
XLA Modules:
  0.0 25.5 jit_solution(9682930131202382294)
XLA Ops:
  1.3 0.1 odd_first_step.1
  1.4 1.3 %collective-permute-start.2 = (f32[528,256]{1,0:T(8,128)S(1)}, f32[528,256]{1,0:T(8,128)S(1)}, u32[]{:S(2)}, u32[]{:S(2)}) collective-permute-start(f32[528,256]{1,0:T(8,128)S(1)} %get-tuple-element.43), channel_id=1, source_target_pairs={{1,2},{3,4},{5,6},{7,8},{9,10},{11,12},{13,14},{17,18},{19,20},{21... | collective-permute-start | bytes 1622024 | tf_op jit(solution)/shard_map/ppermute | solution.py:447
  2.7 2.8 %even_first_step.1 = (f32[520,256]{1,0:T(8,128)S(1)}, f32[136,256]{1,0:T(8,128)S(1)}, f32[128,256]{1,0:T(8,128)S(1)}, f32[72,256]{1,0:T(8,128)S(1)}, f32[8,256]{...) custom-call(s32[1]{0:T(128)S(6)} %copy.8.refs_0_, f32[1,2,2,128,256]{4,3,2,1,0:T(8,128)} %refs_1_.3, ...), custom_call_target="tpu_custom_call" | custom-call | flops 805306368 | bytes 2097152 | tf_op jit(solution)/shard_map/even_first_step/pallas_call | solution.py:417
  5.4 1.9 %collective-permute-start = (f32[520,256]{1,0:T(8,128)S(1)}, f32[520,256]{1,0:T(8,128)S(1)}, u32[]{:S(2)}, u32[]{:S(2)}) collective-permute-start(f32[520,256]{1,0:T(8,128)S(1)} %get-tuple-element.35), channel_id=1, source_target_pairs={{0,1},{2,3},{4,5},{6,7},{8,9},{10,11},{12,13},{14,15},{16,17},{18,... | collective-permute-start | bytes 1597448 | tf_op jit(solution)/shard_map/ppermute | solution.py:452
  7.3 2.3 %collective-permute-start.4 = (f32[136,256]{1,0:T(8,128)S(1)}, f32[136,256]{1,0:T(8,128)S(1)}, u32[]{:S(2)}, u32[]{:S(2)}) collective-permute-start(f32[136,256]{1,0:T(8,128)S(1)} %get-tuple-element.36.plane_ref), channel_id=1, source_target_pairs={{2,1},{4,3},{6,5},{8,7},{10,9},{12,11},{14,13},{18,17},{20,19},{22... | collective-permute-start | bytes 417800 | tf_op jit(solution)/shard_map/ppermute | solution.py:453
  9.6 0.0 collective-permute-done.state_in_ref
  9.6 1.3 %collective-permute-start.1 = (f32[536,256]{1,0:T(8,128)S(1)}, f32[536,256]{1,0:T(8,128)S(1)}, u32[]{:S(2)}, u32[]{:S(2)}) collective-permute-start(f32[536,256]{1,0:T(8,128)S(1)} %get-tuple-element.42.state_in_ref), channel_id=1, source_target_pairs={{1,2},{3,4},{5,6},{7,8},{9,10},{11,12},{13,14},{17,18},{19,20},{21... | collective-permute-start | bytes 1646600 | tf_op jit(solution)/shard_map/ppermute | solution.py:458
  10.9 2.4 %collective-permute-done.2.state_in_ref = f32[528,256]{1,0:T(8,128)S(1)} collective-permute-done((f32[528,256]{1,0:T(8,128)S(1)}, f32[528,256]{1,0:T(8,128)S(1)}, u32[]{:S(2)}, u32[]{:S(2)}) %collective-permute-start.2) | collective-permute-done | bytes 540704 | tf_op jit(solution)/shard_map/ppermute | solution.py:447
  13.3 1.4 %even_arrival_step.1 = (f32[520,256]{1,0:T(8,128)S(1)}, f32[128,256]{1,0:T(8,128)S(1)}, f32[144,256]{1,0:T(8,128)S(1)}) custom-call(f32[528,256]{1,0:T(8,128)S(1)} %collective-permute-done.2.state_in_ref, f32[136,256]{1,0:T(8,128)S(1)} %get-tuple-element.36.plane_ref, f32[128,256]{1,0:T(8,128)S(1)} %get-tuple-element.44.image_in_ref, ...), custom_call_target="tpu_custom_call" | custom-call | flops 805306368 | bytes 2097152 | tf_op jit(solution)/shard_map/even_arrival_step/pallas_call | solution.py:417
  14.7 1.3 %collective-permute-start.3 = (f32[520,256]{1,0:T(8,128)S(1)}, f32[520,256]{1,0:T(8,128)S(1)}, u32[]{:S(2)}, u32[]{:S(2)}) collective-permute-start(f32[520,256]{1,0:T(8,128)S(1)} %get-tuple-element.46), channel_id=1, source_target_pairs={{0,1},{2,3},{4,5},{6,7},{8,9},{10,11},{12,13},{14,15},{16,17},{18,... | collective-permute-start | bytes 1597448 | tf_op jit(solution)/shard_map/ppermute | solution.py:463
  16.0 1.5 %collective-permute-start.5 = (f32[144,256]{1,0:T(8,128)S(1)}, f32[144,256]{1,0:T(8,128)S(1)}, u32[]{:S(2)}, u32[]{:S(2)}) collective-permute-start(f32[144,256]{1,0:T(8,128)S(1)} %get-tuple-element.50), channel_id=1, source_target_pairs={{2,1},{4,3},{6,5},{8,7},{10,9},{12,11},{14,13},{18,17},{20,19},{22... | collective-permute-start | bytes 442376 | tf_op jit(solution)/shard_map/ppermute | solution.py:464
  17.5 0.0 collective-permute-done.4.plane_ref
  17.5 0.0 collective-permute-done.3.state_in_ref
  17.6 1.3 %collective-permute-start.6 = (f32[136,256]{1,0:T(8,128)S(1)}, f32[136,256]{1,0:T(8,128)S(1)}, u32[]{:S(2)}, u32[]{:S(2)}) collective-permute-start(f32[136,256]{1,0:T(8,128)S(1)} %get-tuple-element.47.odd_raw_ref), channel_id=1, source_target_pairs={{1,2},{3,4},{5,6},{7,8},{9,10},{11,12},{13,14},{17,18},{19,20},{21... | collective-permute-start | bytes 417800 | tf_op jit(solution)/shard_map/ppermute | solution.py:473
  18.9 2.5 %collective-permute-done.1.state_in_ref = f32[536,256]{1,0:T(8,128)S(1)} collective-permute-done((f32[536,256]{1,0:T(8,128)S(1)}, f32[536,256]{1,0:T(8,128)S(1)}, u32[]{:S(2)}, u32[]{:S(2)}) %collective-permute-start.1) | collective-permute-done | bytes 548896 | tf_op jit(solution)/shard_map/ppermute | solution.py:458
  21.4 1.4 %even_last_step.1 = (f32[512,256]{1,0:T(8,128)S(1)}, f32[128,256]{1,0:T(8,128)S(1)}, f32[128,256]{1,0:T(8,128)S(1)}) custom-call(f32[536,256]{1,0:T(8,128)S(1)} %collective-permute-done.1.state_in_ref, f32[136,256]{1,0:T(8,128)S(1)} %get-tuple-element.36.plane_ref, f32[128,256]{1,0:T(8,128)S(1)} %get-tuple-element.45.image_in_ref, ...), custom_call_target="tpu_custom_call" | custom-call | tf_op jit(solution)/shard_map/even_last_step/pallas_call | solution.py:417
  22.8 0.1 collective-permute-start.7
  22.9 0.8 %write_fields.1 = (f32[1,2,2,128,256]{4,3,2,1,0:T(8,128)}, f32[8,128]{1,0:T(8,128)S(1)}) custom-call(f32[512,256]{1,0:T(8,128)S(1)} %get-tuple-element.52.odd_ref, f32[512,256]{1,0:T(8,128)S(1)} %get-tuple-element.53.even_ref), custom_call_target="tpu_custom_call" | custom-call | tf_op jit(solution)/shard_map/write_fields/pallas_call | solution.py:417
  23.7 0.0 collective-permute-done.5.below_ref
  23.7 0.5 %collective-permute-done.7.swap_ref = f32[128,256]{1,0:T(8,128)S(1)} collective-permute-done((f32[128,256]{1,0:T(8,128)S(1)}, f32[128,256]{1,0:T(8,128)S(1)}, u32[]{:S(2)}, u32[]{:S(2)}) %collective-permute-start.7) | collective-permute-done | bytes 131104 | tf_op jit(solution)/shard_map/ppermute | solution.py:479
  24.2 0.7 %collective-permute-done.6.above_ref = f32[136,256]{1,0:T(8,128)S(1)} collective-permute-done((f32[136,256]{1,0:T(8,128)S(1)}, f32[136,256]{1,0:T(8,128)S(1)}, u32[]{:S(2)}, u32[]{:S(2)}) %collective-permute-start.6) | collective-permute-done | bytes 139296 | tf_op jit(solution)/shard_map/ppermute | solution.py:473
  24.9 0.7 %image_stencil.1 = f32[1,128,256]{2,1,0:T(8,128)} custom-call(f32[128,256]{1,0:T(8,128)S(1)} %get-tuple-element.49.base_ref, f32[144,256]{1,0:T(8,128)S(1)} %collective-permute-done.5.below_ref, f32[136,256]{1,0:T(8,128)S(1)} %collective-permute-done.6.above_ref, f32[128,256]{1,0:T(8,128)S(1)} %collective-permute-done.7.swap_ref, ...), custom_call_target="tpu_custom_call" | custom-call | tf_op jit(solution)/shard_map/image_stencil/pallas_call | solution.py:417
  (3 shorter events, 0.1 us)
Async XLA Ops:
  1.4 12.0 %collective-permute-start.2 = (f32[528,256]{1,0:T(8,128)S(1)}, f32[528,256]{1,0:T(8,128)S(1)}, u32[]{:S(2)}, u32[]{:S(2)}) collective-permute-start(f32[528,256]{1,0:T(8,128)S(1)} %get-tuple-element.43), channel_id=1, source_target_pairs={{1,2},{3,4},{5,6},{7,8},{9,10},{11,12},{13,14},{17,18},{19,20},{21... | collective-permute-start | bytes 1622024 | tf_op jit(solution)/shard_map/ppermute | solution.py:447
  5.4 4.2 %collective-permute-start = (f32[520,256]{1,0:T(8,128)S(1)}, f32[520,256]{1,0:T(8,128)S(1)}, u32[]{:S(2)}, u32[]{:S(2)}) collective-permute-start(f32[520,256]{1,0:T(8,128)S(1)} %get-tuple-element.35), channel_id=1, source_target_pairs={{0,1},{2,3},{4,5},{6,7},{8,9},{10,11},{12,13},{14,15},{16,17},{18,... | collective-permute-start | bytes 1597448 | tf_op jit(solution)/shard_map/ppermute | solution.py:452
  7.3 10.2 %collective-permute-start.4 = (f32[136,256]{1,0:T(8,128)S(1)}, f32[136,256]{1,0:T(8,128)S(1)}, u32[]{:S(2)}, u32[]{:S(2)}) collective-permute-start(f32[136,256]{1,0:T(8,128)S(1)} %get-tuple-element.36.plane_ref), channel_id=1, source_target_pairs={{2,1},{4,3},{6,5},{8,7},{10,9},{12,11},{14,13},{18,17},{20,19},{22... | collective-permute-start | bytes 417800 | tf_op jit(solution)/shard_map/ppermute | solution.py:453
  9.6 11.8 %collective-permute-start.1 = (f32[536,256]{1,0:T(8,128)S(1)}, f32[536,256]{1,0:T(8,128)S(1)}, u32[]{:S(2)}, u32[]{:S(2)}) collective-permute-start(f32[536,256]{1,0:T(8,128)S(1)} %get-tuple-element.42.state_in_ref), channel_id=1, source_target_pairs={{1,2},{3,4},{5,6},{7,8},{9,10},{11,12},{13,14},{17,18},{19,20},{21... | collective-permute-start | bytes 1646600 | tf_op jit(solution)/shard_map/ppermute | solution.py:458
  14.7 2.9 %collective-permute-start.3 = (f32[520,256]{1,0:T(8,128)S(1)}, f32[520,256]{1,0:T(8,128)S(1)}, u32[]{:S(2)}, u32[]{:S(2)}) collective-permute-start(f32[520,256]{1,0:T(8,128)S(1)} %get-tuple-element.46), channel_id=1, source_target_pairs={{0,1},{2,3},{4,5},{6,7},{8,9},{10,11},{12,13},{14,15},{16,17},{18,... | collective-permute-start | bytes 1597448 | tf_op jit(solution)/shard_map/ppermute | solution.py:463
  16.0 7.7 %collective-permute-start.5 = (f32[144,256]{1,0:T(8,128)S(1)}, f32[144,256]{1,0:T(8,128)S(1)}, u32[]{:S(2)}, u32[]{:S(2)}) collective-permute-start(f32[144,256]{1,0:T(8,128)S(1)} %get-tuple-element.50), channel_id=1, source_target_pairs={{2,1},{4,3},{6,5},{8,7},{10,9},{12,11},{14,13},{18,17},{20,19},{22... | collective-permute-start | bytes 442376 | tf_op jit(solution)/shard_map/ppermute | solution.py:464
  17.6 7.3 %collective-permute-start.6 = (f32[136,256]{1,0:T(8,128)S(1)}, f32[136,256]{1,0:T(8,128)S(1)}, u32[]{:S(2)}, u32[]{:S(2)}) collective-permute-start(f32[136,256]{1,0:T(8,128)S(1)} %get-tuple-element.47.odd_raw_ref), channel_id=1, source_target_pairs={{1,2},{3,4},{5,6},{7,8},{9,10},{11,12},{13,14},{17,18},{19,20},{21... | collective-permute-start | bytes 417800 | tf_op jit(solution)/shard_map/ppermute | solution.py:473
  22.8 1.4 %collective-permute-start.7 = (f32[128,256]{1,0:T(8,128)S(1)}, f32[128,256]{1,0:T(8,128)S(1)}, u32[]{:S(2)}, u32[]{:S(2)}) collective-permute-start(f32[128,256]{1,0:T(8,128)S(1)} %get-tuple-element.51), channel_id=1, source_target_pairs={{0,1},{2,3},{4,5},{6,7},{8,9},{10,11},{12,13},{14,15},{1,0},{3,2},... | collective-permute-start | bytes 393224 | tf_op jit(solution)/shard_map/ppermute | solution.py:479

commit v2 on v1

--- a/solution.py
+++ b/solution.py
@@ -47,10 +47,13 @@
     return views
 
 
-def passes(value, axis):
+def halves(value):
     high = value.astype(jnp.bfloat16)
-    low = (value - high.astype(jnp.float32)).astype(jnp.bfloat16)
-    return jnp.concatenate([high, low, high], axis=axis)
+    return high, (value - high.astype(jnp.float32)).astype(jnp.bfloat16)
+
+
+def dot(left, right):
+    return jnp.dot(left, right, preferred_element_type=jnp.float32)
 
 
 def table_parts(table_ref, turn):
@@ -67,15 +70,19 @@
 
 
 def dot_right(value, table_ref):
-    high, low = table_parts(table_ref, False)
-    return jnp.dot(
-        passes(value, 1), stack(high, high, low), preferred_element_type=jnp.float32
-    )
+    table_high, table_low = table_parts(table_ref, False)
+    high, low = halves(value)
+    both = dot(stack(high, low), table_high)
+    rows = value.shape[0]
+    return both[:rows] + (both[rows:] + dot(high, table_low))
 
 
 def dot_left(table_ref, value):
-    high, low = table_parts(table_ref, True)
-    return jnp.dot(side(high, high, low), passes(value, 0), preferred_element_type=jnp.float32)
+    table_high, table_low = table_parts(table_ref, True)
+    high, low = halves(value)
+    both = dot(stack(table_high, table_low), high)
+    rows = table_high.shape[0]
+    return both[:rows] + (both[rows:] + dot(table_high, low))
 
 
 def cos_sin(angle):
@@ -251,15 +258,9 @@
 
 
 def even_first_kernel(*refs):
-    operands, refs = refs[: 4 + TABLES], refs[4 + TABLES :]
-    kept, refs = refs[: 4 + TABLES], refs[4 + TABLES :]
+    operands, refs = refs[: 4 + TABLES], refs[5 + TABLES :]
     outputs, scratch = refs[: 5 + TABLES], refs[5 + TABLES :]
     pl.when(is_even())(functools.partial(load_and_step, operands, outputs, scratch))
-
-    @pl.when(is_odd())
-    def _():
-        for kept_ref, out_ref in zip(kept, outputs[1:]):
-            out_ref[...] = kept_ref[...]
 
 
 def step_from(state_ref, plane_ref, constants):
@@ -289,10 +290,6 @@
             state_ref[start : start + EXTRA] = state_in_ref[4 * rows :]
         image_ref[...] = image_in_ref[...] + image
 
-    @pl.when(is_even())
-    def _():
-        image_ref[...] = image_in_ref[...]
-
 
 def odd_ahead_kernel(state_in_ref, plane_ref, *refs):
     constants, (image_ref,) = refs[: 2 + TABLES], refs[2 + TABLES :]
@@ -326,10 +323,6 @@
         image = image_in_ref[...] + image
         image_ref[...] = image
         fill_wide(up_ref, image)
-
-    @pl.when(is_odd())
-    def _():
-        image_ref[...] = image_in_ref[...]
 
 
 def odd_last_kernel(state_in_ref, plane_ref, image_in_ref, ahead_ref, *refs):
@@ -405,7 +398,7 @@
     cost = pl.CostEstimate(flops=2 * products, bytes_accessed=16 * rows * cols * 4, transcendentals=0)
 
     long = pl.CostEstimate(
-        flops=10 * 2 * products, bytes_accessed=10 * 16 * rows * cols * 4, transcendentals=0
+        flops=13 * products, bytes_accessed=104 * rows * cols * 4, transcendentals=0
     )
 
     def shape_of(height):
@@ -440,40 +433,40 @@
         pltpu.VMEM((1,) + slowness_table.shape, f32),
         pltpu.SemaphoreType.DMA((4 + TABLES,)),
     ]
-    odd_state, *kept = call(
+    odd_state, odd_plane, odd_image, *odd_constants = call(
         odd_first_kernel, "odd_first_step", operands, [long_state_shape] + kept_shapes,
         in_specs=[hbm] * len(operands), scratch_shapes=scratch,
     )
     from_off = lax.ppermute(odd_state, "slab", off_pairs)
-    even_state, plane, image, *constants = call(
-        even_first_kernel, "even_first_step", (*operands, *kept), [state_shape] + kept_shapes,
-        in_specs=[hbm] * len(operands) + [vmem] * len(kept), scratch_shapes=scratch,
+    even_state, even_plane, even_image, *even_constants = call(
+        even_first_kernel, "even_first_step", (*operands, odd_image), [state_shape] + kept_shapes,
+        in_specs=[hbm] * len(operands) + [vmem], scratch_shapes=scratch,
     )
     from_on = lax.ppermute(even_state, "slab", on_pairs)
-    next_plane = lax.ppermute(plane, "slab", off_back)
-    odd_state, image = call(
-        odd_second_kernel, "odd_second_step", (from_on, plane, image, *constants),
+    next_plane = lax.ppermute(even_plane, "slab", off_back)
+    odd_state, odd_image = call(
+        odd_second_kernel, "odd_second_step", (from_on, odd_plane, odd_image, *odd_constants),
         [shape_of(4 * rows + 3 * EXTRA), image_shape], cost=None,
     )
     last_off = lax.ppermute(odd_state, "slab", off_pairs)
-    even_state, image, up_image = call(
-        even_arrival_kernel, "even_arrival_step", (from_off, plane, image, *constants),
+    even_state, even_image, up_image = call(
+        even_arrival_kernel, "even_arrival_step", (from_off, even_plane, even_image, *even_constants),
         [state_shape, image_shape, shape_of(rows + 2 * EXTRA)],
     )
     last_on = lax.ppermute(even_state, "slab", on_pairs)
     below = lax.ppermute(up_image, "slab", off_back)
     (ahead,) = call(
-        odd_ahead_kernel, "odd_step_ahead", (odd_state, next_plane, *constants), [image_shape],
+        odd_ahead_kernel, "odd_step_ahead", (odd_state, next_plane, *odd_constants), [image_shape],
         cost=long,
     )
     odd_fields, odd_raw, odd_base = call(
-        odd_last_kernel, "odd_last_step", (last_on, plane, image, ahead, *constants),
+        odd_last_kernel, "odd_last_step", (last_on, odd_plane, odd_image, ahead, *odd_constants),
         [shape_of(4 * rows), shape_of(rows + EXTRA), image_shape], cost=None,
     )
     above = lax.ppermute(odd_raw, "slab", off_pairs)
     even_fields, raw, base = call(
         even_last_kernel, "even_last_step",
-        (last_off, plane, image, odd_raw, odd_base, *constants),
+        (last_off, even_plane, even_image, odd_raw, odd_base, *even_constants),
         [shape_of(4 * rows), image_shape, image_shape], cost=None,
     )
     swapped = lax.ppermute(raw, "slab", on_pairs + on_back)

time: 25.8 us -> 25.7 us (level)
    ppermute x1, waiting for transfers between devices: 0.66 us -> 1.15 us  [body(): above = lax.ppermute(odd_raw, 'slab', off_pairs)]
    ppermute x1, waiting for transfers between devices: 0.48 us -> 0.01 us  [body(): swapped = lax.ppermute(raw, 'slab', on_pairs + on_back)]
  transfers between devices with their start and end apart: 8 -> 8, of which waited for: 4 -> 3; matrix products, arithmetic and copies ran while one was open for 0% -> 0% of each run, Pallas kernels for 25% -> 25%
where the time goes in v2:
time: 25.7 us; the launch traced here: 25.5 us
  starting transfers between devices  10.7 us (42%)
  Pallas kernels  7.09 us (28%)
  waiting for transfers between devices  6.19 us (24%)
  between operations  1.42 us (6%)
    pallas_call x9, Pallas kernels, call(): pl.pallas_call(kernel, out_shape=tuple(out_shapes), compiler_params=pltpu...  7.09 us
    ppermute x1, waiting for transfers between devices, body(): last_off = lax.ppermute(odd_state, 'slab', off_pairs)  2.53 us
    ppermute x1, waiting for transfers between devices, body(): from_off = lax.ppermute(odd_state, 'slab', off_pairs)  2.45 us
    ppermute x1, starting transfers between devices, body(): next_plane = lax.ppermute(even_plane, 'slab', off_back)  2.28 us
    ppermute x1, starting transfers between devices, body(): from_on = lax.ppermute(even_state, 'slab', on_pairs)  1.81 us
    ppermute x1, starting transfers between devices, body(): below = lax.ppermute(up_image, 'slab', off_back)  1.39 us
    ppermute x1, starting transfers between devices, body(): last_on = lax.ppermute(even_state, 'slab', on_pairs)  1.32 us
    ppermute x1, starting transfers between devices, body(): from_off = lax.ppermute(odd_state, 'slab', off_pairs)  1.29 us
  transfers between devices with their start and end apart: 8, of which 3 were waited for; matrix products, arithmetic and copies ran while one was open for 0% of the time, Pallas kernels for 25%

profile of v2, /device:TPU:10, one launch (start us, length us, event | category | flops | bytes accessed | tf_op | source)
XLA Modules:
  0.0 25.5 jit_solution(9004310815551914989)
XLA Ops:
  1.3 0.1 odd_first_step.1
  1.4 1.3 %collective-permute-start.2 = (f32[528,256]{1,0:T(8,128)S(1)}, f32[528,256]{1,0:T(8,128)S(1)}, u32[]{:S(2)}, u32[]{:S(2)}) collective-permute-start(f32[528,256]{1,0:T(8,128)S(1)} %get-tuple-element.38), channel_id=1, source_target_pairs={{1,2},{3,4},{5,6},{7,8},{9,10},{11,12},{13,14},{17,18},{19,20},{21... | collective-permute-start | bytes 1622024 | tf_op jit(solution)/shard_map/ppermute | solution.py:440
  2.7 2.7 %even_first_step.1 = (f32[520,256]{1,0:T(8,128)S(1)}, f32[136,256]{1,0:T(8,128)S(1)}, f32[128,256]{1,0:T(8,128)S(1)}, f32[72,256]{1,0:T(8,128)S(1)}, f32[8,256]{...) custom-call(s32[1]{0:T(128)S(6)} %copy.8.refs_0_, f32[1,2,2,128,256]{4,3,2,1,0:T(8,128)} %refs_1_.3, ...), custom_call_target="tpu_custom_call" | custom-call | flops 805306368 | bytes 2097152 | tf_op jit(solution)/shard_map/even_first_step/pallas_call | solution.py:410
  5.4 1.8 %collective-permute-start = (f32[520,256]{1,0:T(8,128)S(1)}, f32[520,256]{1,0:T(8,128)S(1)}, u32[]{:S(2)}, u32[]{:S(2)}) collective-permute-start(f32[520,256]{1,0:T(8,128)S(1)} %get-tuple-element.30), channel_id=1, source_target_pairs={{0,1},{2,3},{4,5},{6,7},{8,9},{10,11},{12,13},{14,15},{16,17},{18,... | collective-permute-start | bytes 1597448 | tf_op jit(solution)/shard_map/ppermute | solution.py:445
  7.2 2.3 %collective-permute-start.4 = (f32[136,256]{1,0:T(8,128)S(1)}, f32[136,256]{1,0:T(8,128)S(1)}, u32[]{:S(2)}, u32[]{:S(2)}) collective-permute-start(f32[136,256]{1,0:T(8,128)S(1)} %get-tuple-element.37.plane_ref), channel_id=1, source_target_pairs={{2,1},{4,3},{6,5},{8,7},{10,9},{12,11},{14,13},{18,17},{20,19},{22... | collective-permute-start | bytes 417800 | tf_op jit(solution)/shard_map/ppermute | solution.py:446
  9.5 0.0 collective-permute-done.state_in_ref
  9.5 1.3 %collective-permute-start.1 = (f32[536,256]{1,0:T(8,128)S(1)}, f32[536,256]{1,0:T(8,128)S(1)}, u32[]{:S(2)}, u32[]{:S(2)}) collective-permute-start(f32[536,256]{1,0:T(8,128)S(1)} %get-tuple-element.36.state_in_ref), channel_id=1, source_target_pairs={{1,2},{3,4},{5,6},{7,8},{9,10},{11,12},{13,14},{17,18},{19,20},{21... | collective-permute-start | bytes 1646600 | tf_op jit(solution)/shard_map/ppermute | solution.py:451
  10.8 2.5 %collective-permute-done.2.state_in_ref = f32[528,256]{1,0:T(8,128)S(1)} collective-permute-done((f32[528,256]{1,0:T(8,128)S(1)}, f32[528,256]{1,0:T(8,128)S(1)}, u32[]{:S(2)}, u32[]{:S(2)}) %collective-permute-start.2) | collective-permute-done | bytes 540704 | tf_op jit(solution)/shard_map/ppermute | solution.py:440
  13.3 1.4 %even_arrival_step.1 = (f32[520,256]{1,0:T(8,128)S(1)}, f32[128,256]{1,0:T(8,128)S(1)}, f32[144,256]{1,0:T(8,128)S(1)}) custom-call(f32[528,256]{1,0:T(8,128)S(1)} %collective-permute-done.2.state_in_ref, f32[136,256]{1,0:T(8,128)S(1)} %get-tuple-element.37.plane_ref, f32[128,256]{1,0:T(8,128)S(1)} %get-tuple-element.39.image_in_ref, ...), custom_call_target="tpu_custom_call" | custom-call | flops 805306368 | bytes 2097152 | tf_op jit(solution)/shard_map/even_arrival_step/pallas_call | solution.py:410
  14.7 1.3 %collective-permute-start.3 = (f32[520,256]{1,0:T(8,128)S(1)}, f32[520,256]{1,0:T(8,128)S(1)}, u32[]{:S(2)}, u32[]{:S(2)}) collective-permute-start(f32[520,256]{1,0:T(8,128)S(1)} %get-tuple-element.45), channel_id=1, source_target_pairs={{0,1},{2,3},{4,5},{6,7},{8,9},{10,11},{12,13},{14,15},{16,17},{18,... | collective-permute-start | bytes 1597448 | tf_op jit(solution)/shard_map/ppermute | solution.py:456
  16.0 1.4 %collective-permute-start.5 = (f32[144,256]{1,0:T(8,128)S(1)}, f32[144,256]{1,0:T(8,128)S(1)}, u32[]{:S(2)}, u32[]{:S(2)}) collective-permute-start(f32[144,256]{1,0:T(8,128)S(1)} %get-tuple-element.50), channel_id=1, source_target_pairs={{2,1},{4,3},{6,5},{8,7},{10,9},{12,11},{14,13},{18,17},{20,19},{22... | collective-permute-start | bytes 442376 | tf_op jit(solution)/shard_map/ppermute | solution.py:457
  17.4 0.0 collective-permute-done.4.plane_ref
  17.4 0.1 collective-permute-done.3.state_in_ref
  17.5 1.3 %collective-permute-start.6 = (f32[136,256]{1,0:T(8,128)S(1)}, f32[136,256]{1,0:T(8,128)S(1)}, u32[]{:S(2)}, u32[]{:S(2)}) collective-permute-start(f32[136,256]{1,0:T(8,128)S(1)} %get-tuple-element.47.odd_raw_ref), channel_id=1, source_target_pairs={{1,2},{3,4},{5,6},{7,8},{9,10},{11,12},{13,14},{17,18},{19,20},{21... | collective-permute-start | bytes 417800 | tf_op jit(solution)/shard_map/ppermute | solution.py:466
  18.8 2.5 %collective-permute-done.1.state_in_ref = f32[536,256]{1,0:T(8,128)S(1)} collective-permute-done((f32[536,256]{1,0:T(8,128)S(1)}, f32[536,256]{1,0:T(8,128)S(1)}, u32[]{:S(2)}, u32[]{:S(2)}) %collective-permute-start.1) | collective-permute-done | bytes 548896 | tf_op jit(solution)/shard_map/ppermute | solution.py:451
  21.3 1.3 %even_last_step.1 = (f32[512,256]{1,0:T(8,128)S(1)}, f32[128,256]{1,0:T(8,128)S(1)}, f32[128,256]{1,0:T(8,128)S(1)}) custom-call(f32[536,256]{1,0:T(8,128)S(1)} %collective-permute-done.1.state_in_ref, f32[136,256]{1,0:T(8,128)S(1)} %get-tuple-element.37.plane_ref, f32[128,256]{1,0:T(8,128)S(1)} %get-tuple-element.44.image_in_ref, ...), custom_call_target="tpu_custom_call" | custom-call | tf_op jit(solution)/shard_map/even_last_step/pallas_call | solution.py:410
  22.7 0.1 collective-permute-start.7
  22.7 0.8 %write_fields.1 = (f32[1,2,2,128,256]{4,3,2,1,0:T(8,128)}, f32[8,128]{1,0:T(8,128)S(1)}) custom-call(f32[512,256]{1,0:T(8,128)S(1)} %get-tuple-element.52.odd_ref, f32[512,256]{1,0:T(8,128)S(1)} %get-tuple-element.53.even_ref), custom_call_target="tpu_custom_call" | custom-call | tf_op jit(solution)/shard_map/write_fields/pallas_call | solution.py:410
  23.6 0.0 collective-permute-done.5.below_ref
  23.6 1.1 %collective-permute-done.6.above_ref = f32[136,256]{1,0:T(8,128)S(1)} collective-permute-done((f32[136,256]{1,0:T(8,128)S(1)}, f32[136,256]{1,0:T(8,128)S(1)}, u32[]{:S(2)}, u32[]{:S(2)}) %collective-permute-start.6) | collective-permute-done | bytes 139296 | tf_op jit(solution)/shard_map/ppermute | solution.py:466
  24.7 0.0 collective-permute-done.7.swap_ref
  24.7 0.7 %image_stencil.1 = f32[1,128,256]{2,1,0:T(8,128)} custom-call(f32[128,256]{1,0:T(8,128)S(1)} %get-tuple-element.49.base_ref, f32[144,256]{1,0:T(8,128)S(1)} %collective-permute-done.5.below_ref, f32[136,256]{1,0:T(8,128)S(1)} %collective-permute-done.6.above_ref, f32[128,256]{1,0:T(8,128)S(1)} %collective-permute-done.7.swap_ref, ...), custom_call_target="tpu_custom_call" | custom-call | tf_op jit(solution)/shard_map/image_stencil/pallas_call | solution.py:410
  (3 shorter events, 0.0 us)
Async XLA Ops:
  1.4 11.9 %collective-permute-start.2 = (f32[528,256]{1,0:T(8,128)S(1)}, f32[528,256]{1,0:T(8,128)S(1)}, u32[]{:S(2)}, u32[]{:S(2)}) collective-permute-start(f32[528,256]{1,0:T(8,128)S(1)} %get-tuple-element.38), channel_id=1, source_target_pairs={{1,2},{3,4},{5,6},{7,8},{9,10},{11,12},{13,14},{17,18},{19,20},{21... | collective-permute-start | bytes 1622024 | tf_op jit(solution)/shard_map/ppermute | solution.py:440
  5.4 4.1 %collective-permute-start = (f32[520,256]{1,0:T(8,128)S(1)}, f32[520,256]{1,0:T(8,128)S(1)}, u32[]{:S(2)}, u32[]{:S(2)}) collective-permute-start(f32[520,256]{1,0:T(8,128)S(1)} %get-tuple-element.30), channel_id=1, source_target_pairs={{0,1},{2,3},{4,5},{6,7},{8,9},{10,11},{12,13},{14,15},{16,17},{18,... | collective-permute-start | bytes 1597448 | tf_op jit(solution)/shard_map/ppermute | solution.py:445
  7.2 10.2 %collective-permute-start.4 = (f32[136,256]{1,0:T(8,128)S(1)}, f32[136,256]{1,0:T(8,128)S(1)}, u32[]{:S(2)}, u32[]{:S(2)}) collective-permute-start(f32[136,256]{1,0:T(8,128)S(1)} %get-tuple-element.37.plane_ref), channel_id=1, source_target_pairs={{2,1},{4,3},{6,5},{8,7},{10,9},{12,11},{14,13},{18,17},{20,19},{22... | collective-permute-start | bytes 417800 | tf_op jit(solution)/shard_map/ppermute | solution.py:446
  9.5 11.8 %collective-permute-start.1 = (f32[536,256]{1,0:T(8,128)S(1)}, f32[536,256]{1,0:T(8,128)S(1)}, u32[]{:S(2)}, u32[]{:S(2)}) collective-permute-start(f32[536,256]{1,0:T(8,128)S(1)} %get-tuple-element.36.state_in_ref), channel_id=1, source_target_pairs={{1,2},{3,4},{5,6},{7,8},{9,10},{11,12},{13,14},{17,18},{19,20},{21... | collective-permute-start | bytes 1646600 | tf_op jit(solution)/shard_map/ppermute | solution.py:451
  14.7 2.8 %collective-permute-start.3 = (f32[520,256]{1,0:T(8,128)S(1)}, f32[520,256]{1,0:T(8,128)S(1)}, u32[]{:S(2)}, u32[]{:S(2)}) collective-permute-start(f32[520,256]{1,0:T(8,128)S(1)} %get-tuple-element.45), channel_id=1, source_target_pairs={{0,1},{2,3},{4,5},{6,7},{8,9},{10,11},{12,13},{14,15},{16,17},{18,... | collective-permute-start | bytes 1597448 | tf_op jit(solution)/shard_map/ppermute | solution.py:456
  16.0 7.6 %collective-permute-start.5 = (f32[144,256]{1,0:T(8,128)S(1)}, f32[144,256]{1,0:T(8,128)S(1)}, u32[]{:S(2)}, u32[]{:S(2)}) collective-permute-start(f32[144,256]{1,0:T(8,128)S(1)} %get-tuple-element.50), channel_id=1, source_target_pairs={{2,1},{4,3},{6,5},{8,7},{10,9},{12,11},{14,13},{18,17},{20,19},{22... | collective-permute-start | bytes 442376 | tf_op jit(solution)/shard_map/ppermute | solution.py:457
  17.5 7.3 %collective-permute-start.6 = (f32[136,256]{1,0:T(8,128)S(1)}, f32[136,256]{1,0:T(8,128)S(1)}, u32[]{:S(2)}, u32[]{:S(2)}) collective-permute-start(f32[136,256]{1,0:T(8,128)S(1)} %get-tuple-element.47.odd_raw_ref), channel_id=1, source_target_pairs={{1,2},{3,4},{5,6},{7,8},{9,10},{11,12},{13,14},{17,18},{19,20},{21... | collective-permute-start | bytes 417800 | tf_op jit(solution)/shard_map/ppermute | solution.py:466
  22.7 2.1 %collective-permute-start.7 = (f32[128,256]{1,0:T(8,128)S(1)}, f32[128,256]{1,0:T(8,128)S(1)}, u32[]{:S(2)}, u32[]{:S(2)}) collective-permute-start(f32[128,256]{1,0:T(8,128)S(1)} %get-tuple-element.51), channel_id=1, source_target_pairs={{0,1},{2,3},{4,5},{6,7},{8,9},{10,11},{12,13},{14,15},{1,0},{3,2},... | collective-permute-start | bytes 393224 | tf_op jit(solution)/shard_map/ppermute | solution.py:472

commit v3 on v2

--- a/solution.py
+++ b/solution.py
@@ -72,9 +72,7 @@
 def dot_right(value, table_ref):
     table_high, table_low = table_parts(table_ref, False)
     high, low = halves(value)
-    both = dot(stack(high, low), table_high)
-    rows = value.shape[0]
-    return both[:rows] + (both[rows:] + dot(high, table_low))
+    return dot(side(high, low, high), stack(table_high, table_high, table_low))
 
 
 def dot_left(table_ref, value):

time: 25.7 us -> 25.7 us (level)
  no operation moved by 1% of the time
where the time goes in v3:
time: 25.7 us; the launch traced here: 25.5 us
  starting transfers between devices  10.8 us (42%)
  Pallas kernels  7.1 us (28%)
  waiting for transfers between devices  6.18 us (24%)
  between operations  1.42 us (6%)
    pallas_call x9, Pallas kernels, call(): pl.pallas_call(kernel, out_shape=tuple(out_shapes), compiler_params=pltpu...  7.1 us
    ppermute x1, waiting for transfers between devices, body(): last_off = lax.ppermute(odd_state, 'slab', off_pairs)  2.54 us
    ppermute x1, waiting for transfers between devices, body(): from_off = lax.ppermute(odd_state, 'slab', off_pairs)  2.45 us
    ppermute x1, starting transfers between devices, body(): next_plane = lax.ppermute(even_plane, 'slab', off_back)  2.28 us
    ppermute x1, starting transfers between devices, body(): from_on = lax.ppermute(even_state, 'slab', on_pairs)  1.83 us
    ppermute x1, starting transfers between devices, body(): below = lax.ppermute(up_image, 'slab', off_back)  1.4 us
    ppermute x1, starting transfers between devices, body(): last_on = lax.ppermute(even_state, 'slab', on_pairs)  1.32 us
    ppermute x1, starting transfers between devices, body(): last_off = lax.ppermute(odd_state, 'slab', off_pairs)  1.29 us
  transfers between devices with their start and end apart: 8, of which 3 were waited for; matrix products, arithmetic and copies ran while one was open for 0% of the time, Pallas kernels for 25%

profile of v3, /device:TPU:10, one launch (start us, length us, event | category | flops | bytes accessed | tf_op | source)
XLA Modules:
  0.0 25.5 jit_solution(12758284403748793111)
XLA Ops:
  1.3 0.1 odd_first_step.1
  1.4 1.3 %collective-permute-start.2 = (f32[528,256]{1,0:T(8,128)S(1)}, f32[528,256]{1,0:T(8,128)S(1)}, u32[]{:S(2)}, u32[]{:S(2)}) collective-permute-start(f32[528,256]{1,0:T(8,128)S(1)} %get-tuple-element.38), channel_id=1, source_target_pairs={{1,2},{3,4},{5,6},{7,8},{9,10},{11,12},{13,14},{17,18},{19,20},{21... | collective-permute-start | bytes 1622024 | tf_op jit(solution)/shard_map/ppermute | solution.py:438
  2.7 2.7 %even_first_step.1 = (f32[520,256]{1,0:T(8,128)S(1)}, f32[136,256]{1,0:T(8,128)S(1)}, f32[128,256]{1,0:T(8,128)S(1)}, f32[72,256]{1,0:T(8,128)S(1)}, f32[8,256]{...) custom-call(s32[1]{0:T(128)S(6)} %copy.8.refs_0_, f32[1,2,2,128,256]{4,3,2,1,0:T(8,128)} %refs_1_.3, ...), custom_call_target="tpu_custom_call" | custom-call | flops 805306368 | bytes 2097152 | tf_op jit(solution)/shard_map/even_first_step/pallas_call | solution.py:408
  5.4 1.8 %collective-permute-start = (f32[520,256]{1,0:T(8,128)S(1)}, f32[520,256]{1,0:T(8,128)S(1)}, u32[]{:S(2)}, u32[]{:S(2)}) collective-permute-start(f32[520,256]{1,0:T(8,128)S(1)} %get-tuple-element.30), channel_id=1, source_target_pairs={{0,1},{2,3},{4,5},{6,7},{8,9},{10,11},{12,13},{14,15},{16,17},{18,... | collective-permute-start | bytes 1597448 | tf_op jit(solution)/shard_map/ppermute | solution.py:443
  7.2 2.3 %collective-permute-start.4 = (f32[136,256]{1,0:T(8,128)S(1)}, f32[136,256]{1,0:T(8,128)S(1)}, u32[]{:S(2)}, u32[]{:S(2)}) collective-permute-start(f32[136,256]{1,0:T(8,128)S(1)} %get-tuple-element.37.plane_ref), channel_id=1, source_target_pairs={{2,1},{4,3},{6,5},{8,7},{10,9},{12,11},{14,13},{18,17},{20,19},{22... | collective-permute-start | bytes 417800 | tf_op jit(solution)/shard_map/ppermute | solution.py:444
  9.5 0.0 collective-permute-done.state_in_ref
  9.6 1.3 %collective-permute-start.1 = (f32[536,256]{1,0:T(8,128)S(1)}, f32[536,256]{1,0:T(8,128)S(1)}, u32[]{:S(2)}, u32[]{:S(2)}) collective-permute-start(f32[536,256]{1,0:T(8,128)S(1)} %get-tuple-element.36.state_in_ref), channel_id=1, source_target_pairs={{1,2},{3,4},{5,6},{7,8},{9,10},{11,12},{13,14},{17,18},{19,20},{21... | collective-permute-start | bytes 1646600 | tf_op jit(solution)/shard_map/ppermute | solution.py:449
  10.9 2.5 %collective-permute-done.2.state_in_ref = f32[528,256]{1,0:T(8,128)S(1)} collective-permute-done((f32[528,256]{1,0:T(8,128)S(1)}, f32[528,256]{1,0:T(8,128)S(1)}, u32[]{:S(2)}, u32[]{:S(2)}) %collective-permute-start.2) | collective-permute-done | bytes 540704 | tf_op jit(solution)/shard_map/ppermute | solution.py:438
  13.3 1.4 %even_arrival_step.1 = (f32[520,256]{1,0:T(8,128)S(1)}, f32[128,256]{1,0:T(8,128)S(1)}, f32[144,256]{1,0:T(8,128)S(1)}) custom-call(f32[528,256]{1,0:T(8,128)S(1)} %collective-permute-done.2.state_in_ref, f32[136,256]{1,0:T(8,128)S(1)} %get-tuple-element.37.plane_ref, f32[128,256]{1,0:T(8,128)S(1)} %get-tuple-element.39.image_in_ref, ...), custom_call_target="tpu_custom_call" | custom-call | flops 805306368 | bytes 2097152 | tf_op jit(solution)/shard_map/even_arrival_step/pallas_call | solution.py:408
  14.7 1.3 %collective-permute-start.3 = (f32[520,256]{1,0:T(8,128)S(1)}, f32[520,256]{1,0:T(8,128)S(1)}, u32[]{:S(2)}, u32[]{:S(2)}) collective-permute-start(f32[520,256]{1,0:T(8,128)S(1)} %get-tuple-element.45), channel_id=1, source_target_pairs={{0,1},{2,3},{4,5},{6,7},{8,9},{10,11},{12,13},{14,15},{16,17},{18,... | collective-permute-start | bytes 1597448 | tf_op jit(solution)/shard_map/ppermute | solution.py:454
  16.0 1.4 %collective-permute-start.5 = (f32[144,256]{1,0:T(8,128)S(1)}, f32[144,256]{1,0:T(8,128)S(1)}, u32[]{:S(2)}, u32[]{:S(2)}) collective-permute-start(f32[144,256]{1,0:T(8,128)S(1)} %get-tuple-element.50), channel_id=1, source_target_pairs={{2,1},{4,3},{6,5},{8,7},{10,9},{12,11},{14,13},{18,17},{20,19},{22... | collective-permute-start | bytes 442376 | tf_op jit(solution)/shard_map/ppermute | solution.py:455
  17.4 0.0 collective-permute-done.4.plane_ref
  17.5 0.0 collective-permute-done.3.state_in_ref
  17.5 1.3 %collective-permute-start.6 = (f32[136,256]{1,0:T(8,128)S(1)}, f32[136,256]{1,0:T(8,128)S(1)}, u32[]{:S(2)}, u32[]{:S(2)}) collective-permute-start(f32[136,256]{1,0:T(8,128)S(1)} %get-tuple-element.47.odd_raw_ref), channel_id=1, source_target_pairs={{1,2},{3,4},{5,6},{7,8},{9,10},{11,12},{13,14},{17,18},{19,20},{21... | collective-permute-start | bytes 417800 | tf_op jit(solution)/shard_map/ppermute | solution.py:464
  18.8 2.5 %collective-permute-done.1.state_in_ref = f32[536,256]{1,0:T(8,128)S(1)} collective-permute-done((f32[536,256]{1,0:T(8,128)S(1)}, f32[536,256]{1,0:T(8,128)S(1)}, u32[]{:S(2)}, u32[]{:S(2)}) %collective-permute-start.1) | collective-permute-done | bytes 548896 | tf_op jit(solution)/shard_map/ppermute | solution.py:449
  21.3 1.4 %even_last_step.1 = (f32[512,256]{1,0:T(8,128)S(1)}, f32[128,256]{1,0:T(8,128)S(1)}, f32[128,256]{1,0:T(8,128)S(1)}) custom-call(f32[536,256]{1,0:T(8,128)S(1)} %collective-permute-done.1.state_in_ref, f32[136,256]{1,0:T(8,128)S(1)} %get-tuple-element.37.plane_ref, f32[128,256]{1,0:T(8,128)S(1)} %get-tuple-element.44.image_in_ref, ...), custom_call_target="tpu_custom_call" | custom-call | tf_op jit(solution)/shard_map/even_last_step/pallas_call | solution.py:408
  22.7 0.1 collective-permute-start.7
  22.8 0.8 %write_fields.1 = (f32[1,2,2,128,256]{4,3,2,1,0:T(8,128)}, f32[8,128]{1,0:T(8,128)S(1)}) custom-call(f32[512,256]{1,0:T(8,128)S(1)} %get-tuple-element.52.odd_ref, f32[512,256]{1,0:T(8,128)S(1)} %get-tuple-element.53.even_ref), custom_call_target="tpu_custom_call" | custom-call | tf_op jit(solution)/shard_map/write_fields/pallas_call | solution.py:408
  23.6 0.0 collective-permute-done.5.below_ref
  23.6 1.1 %collective-permute-done.6.above_ref = f32[136,256]{1,0:T(8,128)S(1)} collective-permute-done((f32[136,256]{1,0:T(8,128)S(1)}, f32[136,256]{1,0:T(8,128)S(1)}, u32[]{:S(2)}, u32[]{:S(2)}) %collective-permute-start.6) | collective-permute-done | bytes 139296 | tf_op jit(solution)/shard_map/ppermute | solution.py:464
  24.8 0.0 collective-permute-done.7.swap_ref
  24.8 0.7 %image_stencil.1 = f32[1,128,256]{2,1,0:T(8,128)} custom-call(f32[128,256]{1,0:T(8,128)S(1)} %get-tuple-element.49.base_ref, f32[144,256]{1,0:T(8,128)S(1)} %collective-permute-done.5.below_ref, f32[136,256]{1,0:T(8,128)S(1)} %collective-permute-done.6.above_ref, f32[128,256]{1,0:T(8,128)S(1)} %collective-permute-done.7.swap_ref, ...), custom_call_target="tpu_custom_call" | custom-call | tf_op jit(solution)/shard_map/image_stencil/pallas_call | solution.py:408
  (3 shorter events, 0.0 us)
Async XLA Ops:
  1.4 12.0 %collective-permute-start.2 = (f32[528,256]{1,0:T(8,128)S(1)}, f32[528,256]{1,0:T(8,128)S(1)}, u32[]{:S(2)}, u32[]{:S(2)}) collective-permute-start(f32[528,256]{1,0:T(8,128)S(1)} %get-tuple-element.38), channel_id=1, source_target_pairs={{1,2},{3,4},{5,6},{7,8},{9,10},{11,12},{13,14},{17,18},{19,20},{21... | collective-permute-start | bytes 1622024 | tf_op jit(solution)/shard_map/ppermute | solution.py:438
  5.4 4.1 %collective-permute-start = (f32[520,256]{1,0:T(8,128)S(1)}, f32[520,256]{1,0:T(8,128)S(1)}, u32[]{:S(2)}, u32[]{:S(2)}) collective-permute-start(f32[520,256]{1,0:T(8,128)S(1)} %get-tuple-element.30), channel_id=1, source_target_pairs={{0,1},{2,3},{4,5},{6,7},{8,9},{10,11},{12,13},{14,15},{16,17},{18,... | collective-permute-start | bytes 1597448 | tf_op jit(solution)/shard_map/ppermute | solution.py:443
  7.2 10.2 %collective-permute-start.4 = (f32[136,256]{1,0:T(8,128)S(1)}, f32[136,256]{1,0:T(8,128)S(1)}, u32[]{:S(2)}, u32[]{:S(2)}) collective-permute-start(f32[136,256]{1,0:T(8,128)S(1)} %get-tuple-element.37.plane_ref), channel_id=1, source_target_pairs={{2,1},{4,3},{6,5},{8,7},{10,9},{12,11},{14,13},{18,17},{20,19},{22... | collective-permute-start | bytes 417800 | tf_op jit(solution)/shard_map/ppermute | solution.py:444
  9.6 11.8 %collective-permute-start.1 = (f32[536,256]{1,0:T(8,128)S(1)}, f32[536,256]{1,0:T(8,128)S(1)}, u32[]{:S(2)}, u32[]{:S(2)}) collective-permute-start(f32[536,256]{1,0:T(8,128)S(1)} %get-tuple-element.36.state_in_ref), channel_id=1, source_target_pairs={{1,2},{3,4},{5,6},{7,8},{9,10},{11,12},{13,14},{17,18},{19,20},{21... | collective-permute-start | bytes 1646600 | tf_op jit(solution)/shard_map/ppermute | solution.py:449
  14.7 2.8 %collective-permute-start.3 = (f32[520,256]{1,0:T(8,128)S(1)}, f32[520,256]{1,0:T(8,128)S(1)}, u32[]{:S(2)}, u32[]{:S(2)}) collective-permute-start(f32[520,256]{1,0:T(8,128)S(1)} %get-tuple-element.45), channel_id=1, source_target_pairs={{0,1},{2,3},{4,5},{6,7},{8,9},{10,11},{12,13},{14,15},{16,17},{18,... | collective-permute-start | bytes 1597448 | tf_op jit(solution)/shard_map/ppermute | solution.py:454
  16.0 7.6 %collective-permute-start.5 = (f32[144,256]{1,0:T(8,128)S(1)}, f32[144,256]{1,0:T(8,128)S(1)}, u32[]{:S(2)}, u32[]{:S(2)}) collective-permute-start(f32[144,256]{1,0:T(8,128)S(1)} %get-tuple-element.50), channel_id=1, source_target_pairs={{2,1},{4,3},{6,5},{8,7},{10,9},{12,11},{14,13},{18,17},{20,19},{22... | collective-permute-start | bytes 442376 | tf_op jit(solution)/shard_map/ppermute | solution.py:455
  17.5 7.3 %collective-permute-start.6 = (f32[136,256]{1,0:T(8,128)S(1)}, f32[136,256]{1,0:T(8,128)S(1)}, u32[]{:S(2)}, u32[]{:S(2)}) collective-permute-start(f32[136,256]{1,0:T(8,128)S(1)} %get-tuple-element.47.odd_raw_ref), channel_id=1, source_target_pairs={{1,2},{3,4},{5,6},{7,8},{9,10},{11,12},{13,14},{17,18},{19,20},{21... | collective-permute-start | bytes 417800 | tf_op jit(solution)/shard_map/ppermute | solution.py:464
  22.7 2.1 %collective-permute-start.7 = (f32[128,256]{1,0:T(8,128)S(1)}, f32[128,256]{1,0:T(8,128)S(1)}, u32[]{:S(2)}, u32[]{:S(2)}) collective-permute-start(f32[128,256]{1,0:T(8,128)S(1)} %get-tuple-element.51), channel_id=1, source_target_pairs={{0,1},{2,3},{4,5},{6,7},{8,9},{10,11},{12,13},{14,15},{1,0},{3,2},... | collective-permute-start | bytes 393224 | tf_op jit(solution)/shard_map/ppermute | solution.py:470

commit v4 on v3

--- a/solution.py
+++ b/solution.py
@@ -78,9 +78,7 @@
 def dot_left(table_ref, value):
     table_high, table_low = table_parts(table_ref, True)
     high, low = halves(value)
-    both = dot(stack(table_high, table_low), high)
-    rows = table_high.shape[0]
-    return both[:rows] + (both[rows:] + dot(table_high, low))
+    return dot(table_high, high) + (dot(table_low, high) + dot(table_high, low))
 
 
 def cos_sin(angle):

time: 25.7 us -> 25.7 us (level)
  transfers between devices with their start and end apart: 8 -> 8, of which waited for: 3 -> 4; matrix products, arithmetic and copies ran while one was open for 0% -> 0% of each run, Pallas kernels for 25% -> 25%
where the time goes in v4:
time: 25.7 us; the launch traced here: 25.5 us
  starting transfers between devices  10.7 us (42%)
  Pallas kernels  7.16 us (28%)
  waiting for transfers between devices  6.18 us (24%)
  between operations  1.42 us (6%)
    pallas_call x9, Pallas kernels, call(): pl.pallas_call(kernel, out_shape=tuple(out_shapes), compiler_params=pltpu...  7.16 us
    ppermute x1, waiting for transfers between devices, body(): last_off = lax.ppermute(odd_state, 'slab', off_pairs)  2.53 us
    ppermute x1, waiting for transfers between devices, body(): from_off = lax.ppermute(odd_state, 'slab', off_pairs)  2.45 us
    ppermute x1, starting transfers between devices, body(): next_plane = lax.ppermute(even_plane, 'slab', off_back)  2.28 us
    ppermute x1, starting transfers between devices, body(): from_on = lax.ppermute(even_state, 'slab', on_pairs)  1.8 us
    ppermute x1, starting transfers between devices, body(): below = lax.ppermute(up_image, 'slab', off_back)  1.39 us
    ppermute x1, starting transfers between devices, body(): last_on = lax.ppermute(even_state, 'slab', on_pairs)  1.32 us
    ppermute x1, starting transfers between devices, body(): from_off = lax.ppermute(odd_state, 'slab', off_pairs)  1.29 us
  transfers between devices with their start and end apart: 8, of which 4 were waited for; matrix products, arithmetic and copies ran while one was open for 0% of the time, Pallas kernels for 25%

profile of v4, /device:TPU:10, one launch (start us, length us, event | category | flops | bytes accessed | tf_op | source)
XLA Modules:
  0.0 25.5 jit_solution(14325120964842002314)
XLA Ops:
  1.3 0.1 odd_first_step.1
  1.4 1.3 %collective-permute-start.2 = (f32[528,256]{1,0:T(8,128)S(1)}, f32[528,256]{1,0:T(8,128)S(1)}, u32[]{:S(2)}, u32[]{:S(2)}) collective-permute-start(f32[528,256]{1,0:T(8,128)S(1)} %get-tuple-element.38), channel_id=1, source_target_pairs={{1,2},{3,4},{5,6},{7,8},{9,10},{11,12},{13,14},{17,18},{19,20},{21... | collective-permute-start | bytes 1622024 | tf_op jit(solution)/shard_map/ppermute | solution.py:436
  2.7 2.8 %even_first_step.1 = (f32[520,256]{1,0:T(8,128)S(1)}, f32[136,256]{1,0:T(8,128)S(1)}, f32[128,256]{1,0:T(8,128)S(1)}, f32[72,256]{1,0:T(8,128)S(1)}, f32[8,256]{...) custom-call(s32[1]{0:T(128)S(6)} %copy.8.refs_0_, f32[1,2,2,128,256]{4,3,2,1,0:T(8,128)} %refs_1_.3, ...), custom_call_target="tpu_custom_call" | custom-call | flops 805306368 | bytes 2097152 | tf_op jit(solution)/shard_map/even_first_step/pallas_call | solution.py:406
  5.4 1.8 %collective-permute-start = (f32[520,256]{1,0:T(8,128)S(1)}, f32[520,256]{1,0:T(8,128)S(1)}, u32[]{:S(2)}, u32[]{:S(2)}) collective-permute-start(f32[520,256]{1,0:T(8,128)S(1)} %get-tuple-element.30), channel_id=1, source_target_pairs={{0,1},{2,3},{4,5},{6,7},{8,9},{10,11},{12,13},{14,15},{16,17},{18,... | collective-permute-start | bytes 1597448 | tf_op jit(solution)/shard_map/ppermute | solution.py:441
  7.2 2.3 %collective-permute-start.4 = (f32[136,256]{1,0:T(8,128)S(1)}, f32[136,256]{1,0:T(8,128)S(1)}, u32[]{:S(2)}, u32[]{:S(2)}) collective-permute-start(f32[136,256]{1,0:T(8,128)S(1)} %get-tuple-element.37.plane_ref), channel_id=1, source_target_pairs={{2,1},{4,3},{6,5},{8,7},{10,9},{12,11},{14,13},{18,17},{20,19},{22... | collective-permute-start | bytes 417800 | tf_op jit(solution)/shard_map/ppermute | solution.py:442
  9.5 0.0 collective-permute-done.state_in_ref
  9.6 1.3 %collective-permute-start.1 = (f32[536,256]{1,0:T(8,128)S(1)}, f32[536,256]{1,0:T(8,128)S(1)}, u32[]{:S(2)}, u32[]{:S(2)}) collective-permute-start(f32[536,256]{1,0:T(8,128)S(1)} %get-tuple-element.36.state_in_ref), channel_id=1, source_target_pairs={{1,2},{3,4},{5,6},{7,8},{9,10},{11,12},{13,14},{17,18},{19,20},{21... | collective-permute-start | bytes 1646600 | tf_op jit(solution)/shard_map/ppermute | solution.py:447
  10.9 2.5 %collective-permute-done.2.state_in_ref = f32[528,256]{1,0:T(8,128)S(1)} collective-permute-done((f32[528,256]{1,0:T(8,128)S(1)}, f32[528,256]{1,0:T(8,128)S(1)}, u32[]{:S(2)}, u32[]{:S(2)}) %collective-permute-start.2) | collective-permute-done | bytes 540704 | tf_op jit(solution)/shard_map/ppermute | solution.py:436
  13.3 1.4 %even_arrival_step.1 = (f32[520,256]{1,0:T(8,128)S(1)}, f32[128,256]{1,0:T(8,128)S(1)}, f32[144,256]{1,0:T(8,128)S(1)}) custom-call(f32[528,256]{1,0:T(8,128)S(1)} %collective-permute-done.2.state_in_ref, f32[136,256]{1,0:T(8,128)S(1)} %get-tuple-element.37.plane_ref, f32[128,256]{1,0:T(8,128)S(1)} %get-tuple-element.39.image_in_ref, ...), custom_call_target="tpu_custom_call" | custom-call | flops 805306368 | bytes 2097152 | tf_op jit(solution)/shard_map/even_arrival_step/pallas_call | solution.py:406
  14.7 1.3 %collective-permute-start.3 = (f32[520,256]{1,0:T(8,128)S(1)}, f32[520,256]{1,0:T(8,128)S(1)}, u32[]{:S(2)}, u32[]{:S(2)}) collective-permute-start(f32[520,256]{1,0:T(8,128)S(1)} %get-tuple-element.45), channel_id=1, source_target_pairs={{0,1},{2,3},{4,5},{6,7},{8,9},{10,11},{12,13},{14,15},{16,17},{18,... | collective-permute-start | bytes 1597448 | tf_op jit(solution)/shard_map/ppermute | solution.py:452
  16.0 1.4 %collective-permute-start.5 = (f32[144,256]{1,0:T(8,128)S(1)}, f32[144,256]{1,0:T(8,128)S(1)}, u32[]{:S(2)}, u32[]{:S(2)}) collective-permute-start(f32[144,256]{1,0:T(8,128)S(1)} %get-tuple-element.50), channel_id=1, source_target_pairs={{2,1},{4,3},{6,5},{8,7},{10,9},{12,11},{14,13},{18,17},{20,19},{22... | collective-permute-start | bytes 442376 | tf_op jit(solution)/shard_map/ppermute | solution.py:453
  17.4 0.0 collective-permute-done.4.plane_ref
  17.5 0.1 collective-permute-done.3.state_in_ref
  17.5 1.3 %collective-permute-start.6 = (f32[136,256]{1,0:T(8,128)S(1)}, f32[136,256]{1,0:T(8,128)S(1)}, u32[]{:S(2)}, u32[]{:S(2)}) collective-permute-start(f32[136,256]{1,0:T(8,128)S(1)} %get-tuple-element.47.odd_raw_ref), channel_id=1, source_target_pairs={{1,2},{3,4},{5,6},{7,8},{9,10},{11,12},{13,14},{17,18},{19,20},{21... | collective-permute-start | bytes 417800 | tf_op jit(solution)/shard_map/ppermute | solution.py:462
  18.8 2.5 %collective-permute-done.1.state_in_ref = f32[536,256]{1,0:T(8,128)S(1)} collective-permute-done((f32[536,256]{1,0:T(8,128)S(1)}, f32[536,256]{1,0:T(8,128)S(1)}, u32[]{:S(2)}, u32[]{:S(2)}) %collective-permute-start.1) | collective-permute-done | bytes 548896 | tf_op jit(solution)/shard_map/ppermute | solution.py:447
  21.3 1.4 %even_last_step.1 = (f32[512,256]{1,0:T(8,128)S(1)}, f32[128,256]{1,0:T(8,128)S(1)}, f32[128,256]{1,0:T(8,128)S(1)}) custom-call(f32[536,256]{1,0:T(8,128)S(1)} %collective-permute-done.1.state_in_ref, f32[136,256]{1,0:T(8,128)S(1)} %get-tuple-element.37.plane_ref, f32[128,256]{1,0:T(8,128)S(1)} %get-tuple-element.44.image_in_ref, ...), custom_call_target="tpu_custom_call" | custom-call | tf_op jit(solution)/shard_map/even_last_step/pallas_call | solution.py:406
  22.7 0.1 collective-permute-start.7
  22.8 0.8 %write_fields.1 = (f32[1,2,2,128,256]{4,3,2,1,0:T(8,128)}, f32[8,128]{1,0:T(8,128)S(1)}) custom-call(f32[512,256]{1,0:T(8,128)S(1)} %get-tuple-element.52.odd_ref, f32[512,256]{1,0:T(8,128)S(1)} %get-tuple-element.53.even_ref), custom_call_target="tpu_custom_call" | custom-call | tf_op jit(solution)/shard_map/write_fields/pallas_call | solution.py:406
  23.6 0.0 collective-permute-done.5.below_ref
  23.6 1.1 %collective-permute-done.6.above_ref = f32[136,256]{1,0:T(8,128)S(1)} collective-permute-done((f32[136,256]{1,0:T(8,128)S(1)}, f32[136,256]{1,0:T(8,128)S(1)}, u32[]{:S(2)}, u32[]{:S(2)}) %collective-permute-start.6) | collective-permute-done | bytes 139296 | tf_op jit(solution)/shard_map/ppermute | solution.py:462
  24.8 0.0 collective-permute-done.7.swap_ref
  24.8 0.7 %image_stencil.1 = f32[1,128,256]{2,1,0:T(8,128)} custom-call(f32[128,256]{1,0:T(8,128)S(1)} %get-tuple-element.49.base_ref, f32[144,256]{1,0:T(8,128)S(1)} %collective-permute-done.5.below_ref, f32[136,256]{1,0:T(8,128)S(1)} %collective-permute-done.6.above_ref, f32[128,256]{1,0:T(8,128)S(1)} %collective-permute-done.7.swap_ref, ...), custom_call_target="tpu_custom_call" | custom-call | tf_op jit(solution)/shard_map/image_stencil/pallas_call | solution.py:406
  (3 shorter events, 0.0 us)
Async XLA Ops:
  1.4 12.0 %collective-permute-start.2 = (f32[528,256]{1,0:T(8,128)S(1)}, f32[528,256]{1,0:T(8,128)S(1)}, u32[]{:S(2)}, u32[]{:S(2)}) collective-permute-start(f32[528,256]{1,0:T(8,128)S(1)} %get-tuple-element.38), channel_id=1, source_target_pairs={{1,2},{3,4},{5,6},{7,8},{9,10},{11,12},{13,14},{17,18},{19,20},{21... | collective-permute-start | bytes 1622024 | tf_op jit(solution)/shard_map/ppermute | solution.py:436
  5.4 4.1 %collective-permute-start = (f32[520,256]{1,0:T(8,128)S(1)}, f32[520,256]{1,0:T(8,128)S(1)}, u32[]{:S(2)}, u32[]{:S(2)}) collective-permute-start(f32[520,256]{1,0:T(8,128)S(1)} %get-tuple-element.30), channel_id=1, source_target_pairs={{0,1},{2,3},{4,5},{6,7},{8,9},{10,11},{12,13},{14,15},{16,17},{18,... | collective-permute-start | bytes 1597448 | tf_op jit(solution)/shard_map/ppermute | solution.py:441
  7.2 10.2 %collective-permute-start.4 = (f32[136,256]{1,0:T(8,128)S(1)}, f32[136,256]{1,0:T(8,128)S(1)}, u32[]{:S(2)}, u32[]{:S(2)}) collective-permute-start(f32[136,256]{1,0:T(8,128)S(1)} %get-tuple-element.37.plane_ref), channel_id=1, source_target_pairs={{2,1},{4,3},{6,5},{8,7},{10,9},{12,11},{14,13},{18,17},{20,19},{22... | collective-permute-start | bytes 417800 | tf_op jit(solution)/shard_map/ppermute | solution.py:442
  9.6 11.8 %collective-permute-start.1 = (f32[536,256]{1,0:T(8,128)S(1)}, f32[536,256]{1,0:T(8,128)S(1)}, u32[]{:S(2)}, u32[]{:S(2)}) collective-permute-start(f32[536,256]{1,0:T(8,128)S(1)} %get-tuple-element.36.state_in_ref), channel_id=1, source_target_pairs={{1,2},{3,4},{5,6},{7,8},{9,10},{11,12},{13,14},{17,18},{19,20},{21... | collective-permute-start | bytes 1646600 | tf_op jit(solution)/shard_map/ppermute | solution.py:447
  14.7 2.8 %collective-permute-start.3 = (f32[520,256]{1,0:T(8,128)S(1)}, f32[520,256]{1,0:T(8,128)S(1)}, u32[]{:S(2)}, u32[]{:S(2)}) collective-permute-start(f32[520,256]{1,0:T(8,128)S(1)} %get-tuple-element.45), channel_id=1, source_target_pairs={{0,1},{2,3},{4,5},{6,7},{8,9},{10,11},{12,13},{14,15},{16,17},{18,... | collective-permute-start | bytes 1597448 | tf_op jit(solution)/shard_map/ppermute | solution.py:452
  16.0 7.6 %collective-permute-start.5 = (f32[144,256]{1,0:T(8,128)S(1)}, f32[144,256]{1,0:T(8,128)S(1)}, u32[]{:S(2)}, u32[]{:S(2)}) collective-permute-start(f32[144,256]{1,0:T(8,128)S(1)} %get-tuple-element.50), channel_id=1, source_target_pairs={{2,1},{4,3},{6,5},{8,7},{10,9},{12,11},{14,13},{18,17},{20,19},{22... | collective-permute-start | bytes 442376 | tf_op jit(solution)/shard_map/ppermute | solution.py:453
  17.5 7.3 %collective-permute-start.6 = (f32[136,256]{1,0:T(8,128)S(1)}, f32[136,256]{1,0:T(8,128)S(1)}, u32[]{:S(2)}, u32[]{:S(2)}) collective-permute-start(f32[136,256]{1,0:T(8,128)S(1)} %get-tuple-element.47.odd_raw_ref), channel_id=1, source_target_pairs={{1,2},{3,4},{5,6},{7,8},{9,10},{11,12},{13,14},{17,18},{19,20},{21... | collective-permute-start | bytes 417800 | tf_op jit(solution)/shard_map/ppermute | solution.py:462
  22.7 2.1 %collective-permute-start.7 = (f32[128,256]{1,0:T(8,128)S(1)}, f32[128,256]{1,0:T(8,128)S(1)}, u32[]{:S(2)}, u32[]{:S(2)}) collective-permute-start(f32[128,256]{1,0:T(8,128)S(1)} %get-tuple-element.51), channel_id=1, source_target_pairs={{0,1},{2,3},{4,5},{6,7},{8,9},{10,11},{12,13},{14,15},{1,0},{3,2},... | collective-permute-start | bytes 393224 | tf_op jit(solution)/shard_map/ppermute | solution.py:468
